TPU v7x, 32 devices: a whole 2x2x4 slice. The times are simulated.
32 devices in a mesh: phase: 4 (over x, core), fsdp: 8 (over z, y).
Axes of the slice: x: 2, y: 2, z: 4, core: 2. Of those that a mesh axis runs over, the one named last changes fastest.
Arguments:
- inputs: bfloat16 [2, 512, 8192], P(None, 'fsdp'), may hold values from -6 to 6
- cotangent: bfloat16 [2, 512, 8192], P(None, 'fsdp'), may hold values from -0.059814453 to 0.059814453
- norm_gain: float32 [4, 8192], P('phase'), may hold values from 0.1 to 1.9
- blocks: bfloat16 [4, 1024, 4096], P('phase', 'fsdp'), may hold values from -0.09375 to 0.09375
- first_moment: float32 [4, 1024, 4096], P('phase', 'fsdp'), may hold values from -9 to 9
- second_moment: float32 [4, 1024, 4096], P('phase', 'fsdp'), may hold values from 0.25 to 4
- row_index: int32 [4, 1024], P('phase', 'fsdp'), may hold values from 0 to 127, as said below
- col_index: int32 [4, 1024], P('phase', 'fsdp'), may hold values from 0 to 15, as said below
- delays: int32 [4], P('phase'), may hold values from 1 to 4
Outputs:
- weight_grad: float32 [4, 1024, 4096], P('phase', 'fsdp')
- gain_grad: float32 [4, 8192], P('phase')
Inputs may be any that keep to these rules, and one draw needn't show every extreme that they name: Within each section the pairs (row_index, col_index) are distinct, so each section has exactly 1024 of its block positions filled. `col_index`: paired with row_index as above.
All inputs are finite; a program needn't handle non-finite values.
Results may differ from a plain program's by a relative error of at most 0.025.
Values may be sent and summed in bfloat16 or wider, within the bound.
A program may use at most 192 MiB of HBM per device.

v0:
```python
import math

import jax
import jax.numpy as jnp
from jax import lax
from jax.sharding import PartitionSpec as P

D = 8192
R = 1024
BLK = 64


learn_rate = 0.002
adam_epsilon = 1e-08
norm_epsilon = 1e-05


def shifted(value, axis, steps):
    count = lax.axis_size(axis)
    initial, last = (max(0, -steps), min(count, count - steps))
    return lax.ppermute(value, axis, [(source, source + steps) for source in range(initial, last)])


def extrapolate(tile_rows, moment_one, moment_two, delay):
    step_size = learn_rate * delay.astype(jnp.float32)
    moved = tile_rows.astype(jnp.float32) - step_size * moment_one / (
        jnp.sqrt(moment_two) + adam_epsilon
    )
    return moved.astype(jnp.bfloat16)


def assemble(tile_rows, row_pick, col_pick):
    stacked = tile_rows.reshape(tile_rows.shape[0], BLK, BLK)
    tile_grid = jnp.zeros((D // BLK, R // BLK, BLK, BLK), jnp.bfloat16)
    tile_grid = tile_grid.at[row_pick, col_pick].set(stacked)
    return tile_grid.transpose(0, 2, 1, 3).reshape(D, R)


def transpose_product(left_side, matrix):
    return lax.dot_general(
        left_side, matrix, (((1,), (1,)), ((), ())), preferred_element_type=jnp.float32
    )


def make_products(tile_flat, row_pick, col_pick):
    matrix = assemble(tile_flat, row_pick, col_pick)

    def times_matrix(left_side):
        return jnp.dot(left_side, matrix, preferred_element_type=jnp.float32)

    def times_transpose(left_side):
        return transpose_product(left_side, matrix)

    return (times_matrix, times_transpose)


def normalize(phase_in, gain_row):
    x_float = phase_in.astype(jnp.float32)
    rms_scale = lax.rsqrt(jnp.mean(x_float * x_float, axis=-1, keepdims=True) + norm_epsilon)
    normed = x_float * rms_scale
    hidden = (normed * gain_row).astype(jnp.bfloat16)
    return (x_float, rms_scale, normed, hidden)


def shards(
    inputs, cotangent, norm_gain, blocks, first_moment, second_moment, row_index, col_index, delays
):
    phases = lax.axis_size("phase")
    phase_id = lax.axis_index("phase")
    micro_count, tok_rows, model_width = inputs.shape
    gain_row = norm_gain[0]
    local_blocks = extrapolate(blocks[0], first_moment[0], second_moment[0], delays[0])
    all_blocks, all_rows, all_cols = (
        lax.all_gather(local_blocks, "fsdp", axis=0, tiled=True),
        lax.all_gather(row_index[0], "fsdp", axis=0, tiled=True),
        lax.all_gather(col_index[0], "fsdp", axis=0, tiled=True),
    )
    forward_matrix, forward_transpose = make_products(all_blocks, all_rows, all_cols)
    tick_count = micro_count + phases - 1

    def forward_compute(tick, incoming, stores):
        batch_index = tick - phase_id
        is_valid = (batch_index >= 0) & (batch_index < micro_count)
        batch_slot = jnp.clip(batch_index, 0, micro_count - 1)
        first_input = lax.dynamic_index_in_dim(inputs, batch_slot, 0, keepdims=False)
        phase_in = jnp.where(phase_id == 0, first_input, incoming)

        def compute(operands):
            phase_in, stores = operands
            x_all, hidden_all, pre_all, act_all = stores
            x_float, rms_scale, normed, hidden = normalize(phase_in, gain_row)
            pre_act = forward_matrix(hidden)
            act_out = jax.nn.silu(pre_act).astype(jnp.bfloat16)
            phase_out = (x_float + forward_transpose(act_out)).astype(jnp.bfloat16)
            x_all = lax.dynamic_update_index_in_dim(x_all, phase_in, batch_slot, 0)
            hidden_all = lax.dynamic_update_index_in_dim(hidden_all, hidden, batch_slot, 0)
            pre_all = lax.dynamic_update_index_in_dim(pre_all, pre_act, batch_slot, 0)
            act_all = lax.dynamic_update_index_in_dim(act_all, act_out, batch_slot, 0)
            return (phase_out, (x_all, hidden_all, pre_all, act_all))

        def forward_passing(operands):
            return operands

        return lax.cond(is_valid, compute, forward_passing, (phase_in, stores))

    def forward_tick(tick, state_carry):
        incoming, stores = state_carry
        phase_out, stores = forward_compute(tick, incoming, stores)
        incoming = shifted(phase_out, "phase", 1)
        return (incoming, stores)

    forward_init = (
        jnp.zeros((micro_count, tok_rows, model_width), jnp.bfloat16),
        jnp.zeros((micro_count, tok_rows, model_width), jnp.bfloat16),
        jnp.zeros((micro_count, tok_rows, R), jnp.float32),
        jnp.zeros((micro_count, tok_rows, R), jnp.bfloat16),
    )
    forward_carry = lax.fori_loop(
        0,
        tick_count - 1,
        forward_tick,
        (jnp.zeros((tok_rows, model_width), jnp.bfloat16), forward_init),
    )
    unused_out, forward_done = forward_compute(tick_count - 1, forward_carry[0], forward_carry[1])
    x_all, hidden_all, pre_all, act_all = forward_done
    back_matrix, back_transpose = (forward_matrix, forward_transpose)

    def backward_compute(tick, incoming, stores):
        batch_index = tick - (phases - 1 - phase_id)
        is_valid = (batch_index >= 0) & (batch_index < micro_count)
        batch_slot = jnp.clip(batch_index, 0, micro_count - 1)
        last_grad = lax.dynamic_index_in_dim(cotangent, batch_slot, 0, keepdims=False)
        grad_out = jnp.where(phase_id == phases - 1, last_grad, incoming)

        def compute(operands):
            grad_out, stores = operands
            grad_all, dpre_all, gain_total = stores
            phase_in = lax.dynamic_index_in_dim(x_all, batch_slot, 0, keepdims=False)
            pre_act = lax.dynamic_index_in_dim(pre_all, batch_slot, 0, keepdims=False)
            x_float, rms_scale, normed, hidden = normalize(phase_in, gain_row)
            dact = back_matrix(grad_out)
            sigmoid_pre = jax.nn.sigmoid(pre_act)
            dpre = (dact * sigmoid_pre * (1.0 + pre_act * (1.0 - sigmoid_pre))).astype(jnp.bfloat16)
            dhidden = back_transpose(dpre)
            gain_total = gain_total + jnp.sum(dhidden * normed, axis=0)
            dnormed = dhidden * gain_row
            inner = jnp.mean(dnormed * normed, axis=-1, keepdims=True)
            grad_in = (
                grad_out.astype(jnp.float32) + rms_scale * (dnormed - normed * inner)
            ).astype(jnp.bfloat16)
            grad_all = lax.dynamic_update_index_in_dim(grad_all, grad_out, batch_slot, 0)
            dpre_all = lax.dynamic_update_index_in_dim(dpre_all, dpre, batch_slot, 0)
            return (grad_in, (grad_all, dpre_all, gain_total))

        def backward_passing(operands):
            return operands

        return lax.cond(is_valid, compute, backward_passing, (grad_out, stores))

    def backward_tick(tick, state_carry):
        incoming, stores = state_carry
        grad_in, stores = backward_compute(tick, incoming, stores)
        incoming = shifted(grad_in, "phase", -1)
        return (incoming, stores)

    backward_init = (
        jnp.zeros((micro_count, tok_rows, model_width), jnp.bfloat16),
        jnp.zeros((micro_count, tok_rows, R), jnp.bfloat16),
        jnp.zeros((model_width,), jnp.float32),
    )
    backward_carry = lax.fori_loop(
        0,
        tick_count - 1,
        backward_tick,
        (jnp.zeros((tok_rows, model_width), jnp.bfloat16), backward_init),
    )
    unused_grad, backward_done = backward_compute(
        tick_count - 1, backward_carry[0], backward_carry[1]
    )
    grad_all, dpre_all, gain_total = backward_done
    token_total = micro_count * tok_rows
    left_cat = jnp.concatenate(
        [hidden_all.reshape(token_total, model_width), grad_all.reshape(token_total, model_width)],
        axis=0,
    )
    right_cat = jnp.concatenate(
        [dpre_all.reshape(token_total, R), act_all.reshape(token_total, R)], axis=0
    )
    left_tiles = left_cat.T.reshape(model_width // BLK, BLK, 2 * token_total)
    right_tiles = right_cat.T.reshape(R // BLK, BLK, 2 * token_total)
    row_count = local_blocks.shape[0] * lax.axis_size("fsdp")
    group_size = math.gcd(row_count, 64)

    def one_group(group_id):
        rows_now = lax.dynamic_slice_in_dim(all_rows, group_id * group_size, group_size)
        cols_now = lax.dynamic_slice_in_dim(all_cols, group_id * group_size, group_size)
        left_rows = jnp.take(left_tiles, rows_now, axis=0)
        right_rows = jnp.take(right_tiles, cols_now, axis=0)
        product = jnp.einsum(
            "nit,njt->nij", left_rows, right_rows, preferred_element_type=jnp.float32
        )
        return product.reshape(group_size, BLK * BLK)

    results = lax.map(one_group, jnp.arange(row_count // group_size, dtype=jnp.int32))
    rounded = lax.optimization_barrier(results.reshape(row_count, BLK * BLK).astype(jnp.bfloat16))
    weight_part = lax.psum_scatter(
        rounded.astype(jnp.float32).astype(jnp.bfloat16), "fsdp", scatter_dimension=0, tiled=True
    ).astype(jnp.float32)
    gain_part = lax.psum(gain_total.astype(jnp.bfloat16), "fsdp").astype(jnp.float32)
    return (weight_part[None], gain_part[None])


def solution(mesh):
    in_specs = (
        P(None, "fsdp", None),
        P(None, "fsdp", None),
        P("phase", None),
        P("phase", "fsdp", None),
        P("phase", "fsdp", None),
        P("phase", "fsdp", None),
        P("phase", "fsdp"),
        P("phase", "fsdp"),
        P("phase"),
    )
    out_specs = (P("phase", "fsdp", None), P("phase", None))
    return jax.shard_map(shards, mesh=mesh, in_specs=in_specs, out_specs=out_specs, check_vma=False)
```

profile of v0, /device:TPU:0, one launch (start us, length us, event | category | flops | bytes accessed | tf_op | source)
XLA Modules:
  0.0 1100.7 jit_solution(1173611312640507033)
XLA Ops:
  18.0 22.3 %all-gather = s32[1,1024]{1,0:T(1,128)S(1)} all-gather(s32[1,128]{1,0:T(1,128)S(1)} %copy-done.11), channel_id=2, replica_groups=mesh['phase'=4,'fsdp'=8] {'fsdp'}, dimensions={1}, use_global_device_ids=true | all-gather | bytes 4608 | tf_op jit(solution)/shard_map/all_gather | solution.py:75
  40.3 16.3 %all-gather.1 = s32[1,1024]{1,0:T(1,128)S(1)} all-gather(s32[1,128]{1,0:T(1,128)S(1)} %copy-done.12), channel_id=3, replica_groups=mesh['phase'=4,'fsdp'=8] {'fsdp'}, dimensions={1}, use_global_device_ids=true | all-gather | bytes 4608 | tf_op jit(solution)/shard_map/all_gather | solution.py:76
  57.2 89.0 %all-gather.5.cloned.1.call-done = bf16[1,1024,4096]{1,2,0:T(8,128)(2,1)} async-done(((bf16[1,128,4096]{1,2,0:T(8,128)(2,1)}), bf16[1,1024,4096]{1,2,0:T(8,128)(2,1)}) %all-gather.5.cloned.1.call-update) | async-done | bytes 8388624 | tf_op jit(solution)/shard_map/all_gather | solution.py:74
  146.2 24.0 %copy.22 = bf16[1024,64,64]{2,1,0:T(8,128)(2,1)} copy(bf16[1024,64,64]{0,2,1:T(8,128)(2,1)} %bitcast.136) | data formatting | bytes 16777216 | tf_op jit(solution)/shard_map/reshape | solution.py:33
  170.2 11.3 %broadcast.128 = bf16[2048,64,64]{2,1,0:T(8,128)(2,1)} broadcast(bf16[]{:T(256)} %constant.268.clone.1), dimensions={} | broadcast | bytes 16777218
  181.4 132.3 %scatter_fusion = bf16[2048,64,64]{2,1,0:T(8,128)(2,1)} fusion(bf16[2048,64,64]{2,1,0:T(8,128)(2,1)} %broadcast.128, s32[1024]{0:T(1024)S(1)} %broadcast_select_fusion, bf16[1024,64,64]{2,1,0:T(8,128)(2,1)} %copy.22), kind=kCustom, calls=%fused_computation.2 | custom fusion | bytes 25169920
  313.8 34.0 %copy.23 = bf16[128,64,16,64]{3,2,1,0:T(8,128)(2,1)} copy(bf16[128,64,16,64]{3,1,2,0:T(8,128)(2,1)} %bitcast.128) | data formatting | bytes 33554432 | tf_op jit(solution)/shard_map/transpose | solution.py:36
  347.8 44.1 %reshape.119 = bf16[8192,1024]{1,0:T(8,128)(2,1)} reshape(bf16[128,64,16,64]{3,2,1,0:T(8,128)(2,1)} %copy.23) | data formatting | bytes 33554432 | tf_op jit(solution)/shard_map/reshape | solution.py:36
  396.0 113.0 %while.53 = (s32[]{:T(128)}, bf16[64,8192]{1,0:T(8,128)(2,1)S(1)}, bf16[2,64,8192]{2,1,0:T(8,128)(2,1)}, bf16[2,64,8192]{2,1,0:T(8,128)(2,1)}, f32[2,64,1024]{2,...) while((s32[]{:T(128)}, bf16[64,8192]{1,0:T(8,128)(2,1)S(1)}, ...), condition=%wide.region_5.6_spmd, body=%wide.region_1.5_spmd.sunk | while | flops 2156003328 | bytes 53675808 | solution.py:118
  397.6 23.1 %conditional.8 = (bf16[64,8192]{1,0:T(8,128)(2,1)S(1)}, bf16[2,64,8192]{2,1,0:T(8,128)(2,1)}, bf16[2,64,8192]{2,1,0:T(8,128)(2,1)}, f32[2,64,1024]{2,1,0:T(8,128)}, bf16[2,64,1024]{2,1,0:T(8,128)(2,1)S(1)}) conditional(s32[]{:T(128)} %convert_element_type.163, (bf16[64,8192]{1,0:T(8,128)(2,1)S(1)}, bf16[2,64,8192]{2,1,0:T(8,128)(2,1)}, ...), branch_computations={%region_2.2_spmd, %region_3.4_spmd} | conditional | flops 2155479040 | bytes 46335432 | solution.py:104
  398.3 9.6 bitcast_dynamic-update-slice_fusion.2
  408.0 11.0 %fusion = bf16[64,8192]{1,0:T(8,128)(2,1)S(1)} fusion(bf16[8192,1024]{1,0:T(8,128)(2,1)} %get-tuple-element.730, bf16[64,8192]{1,0:T(8,128)(2,1)S(1)} %get-tuple-element.728, f32[64,1024]{1,0:T(8,128)S(1)} %get-tuple-element.925), kind=kOutput, calls=%fused_computation.4 | convolution fusion | flops 1075642368 | bytes 19136512 | tf_op jit(solution)/shard_map/while/body/eval_jaxpr/cond/branch_1_fun/dot_general | solution.py:40
  425.6 23.1 %conditional.8 = (bf16[64,8192]{1,0:T(8,128)(2,1)S(1)}, bf16[2,64,8192]{2,1,0:T(8,128)(2,1)}, bf16[2,64,8192]{2,1,0:T(8,128)(2,1)}, f32[2,64,1024]{2,1,0:T(8,128)}, bf16[2,64,1024]{2,1,0:T(8,128)(2,1)S(1)}) conditional(s32[]{:T(128)} %convert_element_type.163, (bf16[64,8192]{1,0:T(8,128)(2,1)S(1)}, bf16[2,64,8192]{2,1,0:T(8,128)(2,1)}, ...), branch_computations={%region_2.2_spmd, %region_3.4_spmd} | conditional | flops 2155479040 | bytes 46335432 | solution.py:104
  426.3 9.6 bitcast_dynamic-update-slice_fusion.2
  436.1 11.0 %fusion = bf16[64,8192]{1,0:T(8,128)(2,1)S(1)} fusion(bf16[8192,1024]{1,0:T(8,128)(2,1)} %get-tuple-element.730, bf16[64,8192]{1,0:T(8,128)(2,1)S(1)} %get-tuple-element.728, f32[64,1024]{1,0:T(8,128)S(1)} %get-tuple-element.925), kind=kOutput, calls=%fused_computation.4 | convolution fusion | flops 1075642368 | bytes 19136512 | tf_op jit(solution)/shard_map/while/body/eval_jaxpr/cond/branch_1_fun/dot_general | solution.py:40
  454.7 34.4 %collective-permute-start = (bf16[64,8192]{1,0:T(8,128)(2,1)S(1)}, bf16[64,8192]{1,0:T(8,128)(2,1)S(1)}, u32[]{:S(2)}, u32[]{:S(2)}) collective-permute-start(bf16[64,8192]{1,0:T(8,128)(2,1)S(1)} %get-tuple-element.1114), channel_id=1, source_target_pairs={{0,8},{8,16},{16,24},{1,9},{9,17},{17,25},{2,10},{10,18},{18,26},{... | collective-permute-start | bytes 3145736 | tf_op jit(solution)/shard_map/while/body/eval_jaxpr/ppermute | solution.py:21
  492.8 13.9 %collective-permute-start = (bf16[64,8192]{1,0:T(8,128)(2,1)S(1)}, bf16[64,8192]{1,0:T(8,128)(2,1)S(1)}, u32[]{:S(2)}, u32[]{:S(2)}) collective-permute-start(bf16[64,8192]{1,0:T(8,128)(2,1)S(1)} %get-tuple-element.1114), channel_id=1, source_target_pairs={{0,8},{8,16},{16,24},{1,9},{9,17},{17,25},{2,10},{10,18},{18,26},{... | collective-permute-start | bytes 3145736 | tf_op jit(solution)/shard_map/while/body/eval_jaxpr/ppermute | solution.py:21
  511.3 186.5 %while.54 = (s32[]{:T(128)}, bf16[64,8192]{1,0:T(8,128)(2,1)S(1)}, bf16[2,64,8192]{2,1,0:T(8,128)(2,1)}, bf16[2,64,1024]{2,1,0:T(8,128)(2,1)S(1)}, f32[8192]{0:T...) while((s32[]{:T(128)}, bf16[64,8192]{1,0:T(8,128)(2,1)S(1)}, ...), condition=%wide.region_15.16_spmd, body=%wide.region_9.15_spmd.sunk | while | flops 2158559232 | bytes 56429296 | solution.py:171
  515.2 37.9 %collective-permute-done.1 = bf16[64,8192]{1,0:T(8,128)(2,1)S(1)} collective-permute-done((bf16[64,8192]{1,0:T(8,128)(2,1)}, bf16[64,8192]{1,0:T(8,128)(2,1)S(1)}, u32[]{:S(2)}, u32[]{:S(2)}) %collective-permute-start.1) | collective-permute-done | bytes 1048608 | tf_op jit(solution)/shard_map/while/body/eval_jaxpr/ppermute | solution.py:21
  556.7 15.8 %collective-permute-done.1 = bf16[64,8192]{1,0:T(8,128)(2,1)S(1)} collective-permute-done((bf16[64,8192]{1,0:T(8,128)(2,1)}, bf16[64,8192]{1,0:T(8,128)(2,1)S(1)}, u32[]{:S(2)}, u32[]{:S(2)}) %collective-permute-start.1) | collective-permute-done | bytes 1048608 | tf_op jit(solution)/shard_map/while/body/eval_jaxpr/ppermute | solution.py:21
  576.1 78.3 %collective-permute-done.1 = bf16[64,8192]{1,0:T(8,128)(2,1)S(1)} collective-permute-done((bf16[64,8192]{1,0:T(8,128)(2,1)}, bf16[64,8192]{1,0:T(8,128)(2,1)S(1)}, u32[]{:S(2)}, u32[]{:S(2)}) %collective-permute-start.1) | collective-permute-done | bytes 1048608 | tf_op jit(solution)/shard_map/while/body/eval_jaxpr/ppermute | solution.py:21
  655.7 25.8 %conditional.9 = (bf16[64,8192]{1,0:T(8,128)(2,1)}, bf16[2,64,8192]{2,1,0:T(8,128)(2,1)}, bf16[2,64,1024]{2,1,0:T(8,128)(2,1)S(1)}, f32[8192]{0:T(1024)S(1)}) conditional(s32[]{:T(128)} %convert_element_type.164, (bf16[64,8192]{1,0:T(8,128)(2,1)S(1)}, bf16[2,64,8192]{2,1,0:T(8,128)(2,1)}, bf16[2,64,1024]{2,1,0:T(8,128)(2,1)S(1)}, ...), branch_computations={%region_10.10_spmd, %region_11.14_spmd} | conditional | flops 2158034944 | bytes 49088912 | solution.py:158
  655.7 8.8 bitcast_dynamic-update-slice_fusion.9
  666.2 11.4 %fusion.19 = (f32[8192]{0:T(1024)S(1)}, f32[64]{0:T(128)S(1)}, f32[64,8192]{1,0:T(8,128)S(1)}) fusion(f32[64]{0:T(128)S(1)} %add_rsqrt_fusion.2, bf16[2,64,8192]{2,1,0:T(8,128)(2,1)} %get-tuple-element.764, s32[]{:T(128)S(6)} %select_n.115, f32[8192]{0:T(1024)S(1)} %bitcast.134, bf16[64,1024]{1,0:T(8,128)(2,1)S(1)} %get-tuple-element.928, ...), kind=kOutput, calls=%fused_computation.41 | convolution fusion | flops 1077403648 | bytes 20120068 | tf_op jit(solution)/shard_map/while/body/eval_jaxpr/cond/branch_1_fun/dot_general | solution.py:40
  682.8 15.0 %collective-permute-done.1 = bf16[64,8192]{1,0:T(8,128)(2,1)S(1)} collective-permute-done((bf16[64,8192]{1,0:T(8,128)(2,1)}, bf16[64,8192]{1,0:T(8,128)(2,1)S(1)}, u32[]{:S(2)}, u32[]{:S(2)}) %collective-permute-start.1) | collective-permute-done | bytes 1048608 | tf_op jit(solution)/shard_map/while/body/eval_jaxpr/ppermute | solution.py:21
  697.9 24.3 %conditional.5 = (f32[8192]{0:T(1024)S(1)}, bf16[128,8192]{1,0:T(8,128)(2,1)}, bf16[128,1024]{1,0:T(8,128)(2,1)S(1)}) conditional(s32[]{:T(128)} %convert_element_type.103, (f32[8192]{0:T(1024)S(1)}, bf16[2,64,8192]{2,1,0:T(8,128)(2,1)}, bf16[2,64,1024]{2,1,0:T(8,128)(2,1)S(1)}) %tuple.183, (pred[]{:T(512)}, s32[]{:T(128)}, ...), branch_computations={%region_16.17_spmd, %region_17.20_spmd} | conditional | flops 2152792064 | bytes 41684028 | solution.py:158
  697.9 9.1 bitcast_dynamic-update-slice_fusion.11
  708.5 11.2 %fusion.28 = f32[8192]{0:T(1024)S(1)} fusion(bf16[64,1024]{1,0:T(8,128)(2,1)S(1)} %get-tuple-element.930, bf16[8192,1024]{1,0:T(8,128)(2,1)} %get-tuple-element.794, f32[64]{0:T(128)S(1)} %add_rsqrt_fusion.3, bf16[2,64,8192]{2,1,0:T(8,128)(2,1)} %get-tuple-element.796, s32[]{:T(128)S(6)} %min.25), kind=kOutput, calls=%fused_computation.61 | convolution fusion | flops 1075830784 | bytes 17989892 | tf_op jit(solution)/shard_map/cond/branch_1_fun/dot_general | solution.py:40
  727.1 6.4 copy.24
  733.4 211.1 %while.55 = (s32[]{:T(128)}, bf16[16,64,4096]{2,1,0:T(8,128)(2,1)}, s32[16]{0:T(128)S(1)}, s32[1024]{0:T(1024)}, bf16[128,64,256]{2,1,0:T(8,128)(2,1)}, /*index=...) while((s32[]{:T(128)}, bf16[16,64,4096]{2,1,0:T(8,128)(2,1)}, ...), condition=%wide.region_21.22_spmd, body=%wide.region_20.21_spmd.sunk | while | flops 136317696 | bytes 15215531 | solution.py:204
  944.6 35.9 %psum.7 = bf16[1,8192]{1,0:T(2,128)(2,1)S(1)} all-reduce(bf16[1,8192]{1,0:T(2,128)(2,1)S(1)} %broadcast_in_dim.120), channel_id=1, replica_groups=mesh['phase'=4,'fsdp'=8] {'fsdp'}, use_global_device_ids=true, to_apply=%region_23.24 | all-reduce | flops 8192 | bytes 32768 | tf_op jit(solution)/shard_map/psum | solution.py:209
  981.2 109.9 %reduce-scatter.2.cloned.1.call-done = bf16[128,4096]{1,0:T(8,128)(2,1)} async-done(((bf16[1024,4096]{1,0:T(8,128)(2,1)}), bf16[128,4096]{1,0:T(8,128)(2,1)}) %reduce-scatter.2.cloned.1.call-update) | async-done | bytes 1048592 | tf_op jit(solution)/shard_map/reduce_scatter | solution.py:206
  (260 shorter events, 274.3 us)
Async XLA Ops:
  7.2 139.0 %all-gather.5.cloned.1.call-start = ((), (), s32[]{:S(2)}) async-start(), calls=%async_computation.2 | async-start | bytes 9437184 | tf_op jit(solution)/shard_map/all_gather | solution.py:74
  14.3 3.7 copy-start.11
  14.3 26.0 %copy-start.12 = (s32[1,128]{1,0:T(1,128)S(1)}, s32[1,128]{1,0:T(1,128)}, u32[]{:S(2)}) copy-start(s32[1,128]{1,0:T(1,128)} %param.30) | copy-start | bytes 1540
  14.3 42.3 %copy-start.14 = (s32[2]{0:T(128)S(1)}, s32[2]{0:T(128)}, u32[]{:S(2)}) copy-start(s32[2]{0:T(128)} %constant.281) | copy-start | bytes 28
  14.3 42.4 %copy-start.13 = (s32[2]{0:T(128)S(1)}, s32[2]{0:T(128)}, u32[]{:S(2)}) copy-start(s32[2]{0:T(128)} %constant.284) | copy-start | bytes 28
  17.9 1073.2 %reduce-scatter.2.cloned.1.call-start = ((), (), s32[]{:S(2)}) async-start(), calls=%async_computation.1 | async-start | bytes 9437184 | tf_op jit(solution)/shard_map/reduce_scatter | solution.py:206
  40.3 16.3 %copy-start.9 = (s32[1,1024]{1,0:T(1,128)}, s32[1,1024]{1,0:T(1,128)S(1)}, u32[]{:S(2)}) copy-start(s32[1,1024]{1,0:T(1,128)S(1)} %all-gather) | copy-start | bytes 12292
  56.6 0.6 copy-start.10
  393.5 2.5 copy-start
  397.6 0.7 copy-start.1
  398.3 9.6 copy-start.2
  408.0 11.0 %copy-start.3 = (bf16[2,64,1024]{2,1,0:T(8,128)(2,1)}, bf16[2,64,1024]{2,1,0:T(8,128)(2,1)S(1)}, u32[]{:S(2)}) copy-start(bf16[2,64,1024]{2,1,0:T(8,128)(2,1)S(1)} %bitcast_dynamic-update-slice_fusion.3) | copy-start | bytes 786436 | tf_op jit(solution)/shard_map/while/body/eval_jaxpr/cond
  419.1 1.7 copy-start.4
  420.7 3.6 collective-permute-start
  425.6 0.7 copy-start.1
  426.3 9.6 copy-start.2
  436.0 11.0 %copy-start.3 = (bf16[2,64,1024]{2,1,0:T(8,128)(2,1)}, bf16[2,64,1024]{2,1,0:T(8,128)(2,1)S(1)}, u32[]{:S(2)}) copy-start(bf16[2,64,1024]{2,1,0:T(8,128)(2,1)S(1)} %bitcast_dynamic-update-slice_fusion.3) | copy-start | bytes 786436 | tf_op jit(solution)/shard_map/while/body/eval_jaxpr/cond
  447.1 1.6 copy-start.4
  448.7 4.6 collective-permute-start
  454.7 36.7 %collective-permute-start = (bf16[64,8192]{1,0:T(8,128)(2,1)S(1)}, bf16[64,8192]{1,0:T(8,128)(2,1)S(1)}, u32[]{:S(2)}, u32[]{:S(2)}) collective-permute-start(bf16[64,8192]{1,0:T(8,128)(2,1)S(1)} %get-tuple-element.1114), channel_id=1, source_target_pairs={{0,8},{8,16},{16,24},{1,9},{9,17},{17,25},{2,10},{10,18},{18,26},{... | collective-permute-start | bytes 3145736 | tf_op jit(solution)/shard_map/while/body/eval_jaxpr/ppermute | solution.py:21
  492.8 16.1 %collective-permute-start = (bf16[64,8192]{1,0:T(8,128)(2,1)S(1)}, bf16[64,8192]{1,0:T(8,128)(2,1)S(1)}, u32[]{:S(2)}, u32[]{:S(2)}) collective-permute-start(bf16[64,8192]{1,0:T(8,128)(2,1)S(1)} %get-tuple-element.1114), channel_id=1, source_target_pairs={{0,8},{8,16},{16,24},{1,9},{9,17},{17,25},{2,10},{10,18},{18,26},{... | collective-permute-start | bytes 3145736 | tf_op jit(solution)/shard_map/while/body/eval_jaxpr/ppermute | solution.py:21
  509.0 0.7 copy-start.5
  513.9 39.2 %collective-permute-start.1 = (bf16[64,8192]{1,0:T(8,128)(2,1)}, bf16[64,8192]{1,0:T(8,128)(2,1)S(1)}, u32[]{:S(2)}, u32[]{:S(2)}) collective-permute-start(bf16[64,8192]{1,0:T(8,128)(2,1)} %get-tuple-element.1131), channel_id=1, source_target_pairs={{8,0},{16,8},{24,16},{9,1},{17,9},{25,17},{10,2},{18,10},{26,18},{... | collective-permute-start | bytes 3145736 | tf_op jit(solution)/shard_map/while/body/eval_jaxpr/ppermute | solution.py:21
  555.4 17.1 %collective-permute-start.1 = (bf16[64,8192]{1,0:T(8,128)(2,1)}, bf16[64,8192]{1,0:T(8,128)(2,1)S(1)}, u32[]{:S(2)}, u32[]{:S(2)}) collective-permute-start(bf16[64,8192]{1,0:T(8,128)(2,1)} %get-tuple-element.1131), channel_id=1, source_target_pairs={{8,0},{16,8},{24,16},{9,1},{17,9},{25,17},{10,2},{18,10},{26,18},{... | collective-permute-start | bytes 3145736 | tf_op jit(solution)/shard_map/while/body/eval_jaxpr/ppermute | solution.py:21
  574.8 79.6 %collective-permute-start.1 = (bf16[64,8192]{1,0:T(8,128)(2,1)}, bf16[64,8192]{1,0:T(8,128)(2,1)S(1)}, u32[]{:S(2)}, u32[]{:S(2)}) collective-permute-start(bf16[64,8192]{1,0:T(8,128)(2,1)} %get-tuple-element.1131), channel_id=1, source_target_pairs={{8,0},{16,8},{24,16},{9,1},{17,9},{25,17},{10,2},{18,10},{26,18},{... | collective-permute-start | bytes 3145736 | tf_op jit(solution)/shard_map/while/body/eval_jaxpr/ppermute | solution.py:21
  664.6 1.7 copy-start.7
  680.5 1.1 copy-start.8
  681.5 16.3 %collective-permute-start.1 = (bf16[64,8192]{1,0:T(8,128)(2,1)}, bf16[64,8192]{1,0:T(8,128)(2,1)S(1)}, u32[]{:S(2)}, u32[]{:S(2)}) collective-permute-start(bf16[64,8192]{1,0:T(8,128)(2,1)} %get-tuple-element.1131), channel_id=1, source_target_pairs={{8,0},{16,8},{24,16},{9,1},{17,9},{25,17},{10,2},{18,10},{26,18},{... | collective-permute-start | bytes 3145736 | tf_op jit(solution)/shard_map/while/body/eval_jaxpr/ppermute | solution.py:21
  697.9 24.3 %copy-start.6 = (bf16[128,1024]{1,0:T(8,128)(2,1)S(1)}, bf16[128,1024]{1,0:T(8,128)(2,1)}, u32[]{:S(2)}) copy-start(bf16[128,1024]{1,0:T(8,128)(2,1)} %copy-done.5) | copy-start | bytes 786436
Sparse Core Ops, SparseCore 0:
  18.0 128.1 all-gather.4
  944.7 146.3 reduce-scatter.1
where the time goes:
time: 1110 us; the launch traced here: 1100 us
  local copies, waits for them, and re-layouts  404 us (36%)
  waiting for transfers between devices  355 us (32%)
  matrix products  135 us (12%)
  blocking collectives  74.5 us (7%)
  starting transfers between devices  57.3 us (5%)
  other arithmetic  48 us (4%)
  between operations  14.9 us (1%)
  loops' own time  11.9 us (1%)
    ppermute x8, waiting for transfers between devices, shifted(): lax.ppermute(value, axis, [(source, source + steps) for source in range(i...  156 us
    unnamed x23, local copies, waits for them, and re-layouts  151 us
    reduce_scatter x1, waiting for transfers between devices, shards(): lax.psum_scatter(rounded.astype(jnp.float32).astype(jnp.bfloat16), 'fsdp'...  110 us
    all_gather x1, waiting for transfers between devices, shards(): lax.all_gather(local_blocks, 'fsdp', axis=0, tiled=True)  89 us
    gather x16, local copies, waits for them, and re-layouts, one_group(): left_rows = jnp.take(left_tiles, rows_now, axis=0)  67 us
    ppermute x8, starting transfers between devices, shifted(): lax.ppermute(value, axis, [(source, source + steps) for source in range(i...  57.2 us
    dot_general x16, matrix products, one_group(): jnp.einsum('nit,njt->nij', left_rows, right_rows, preferred_element_type=...  53.4 us
    dot_general x4, matrix products, transpose_product(): lax.dot_general(left_side, matrix, (((1,), (1,)), ((), ())), preferred_el...  44.7 us
  transfers between devices with their start and end apart: 10, of which 10 were waited for; matrix products, arithmetic and copies ran while one was open for 0% of the time, Pallas kernels for 0%

commit v1 on v0

--- a/solution.py
+++ b/solution.py
@@ -1,13 +1,16 @@
-import math
+import functools
 
 import jax
 import jax.numpy as jnp
 from jax import lax
+from jax.experimental import pallas as pl
+from jax.experimental.pallas import tpu as pltpu
 from jax.sharding import PartitionSpec as P
 
 D = 8192
 R = 1024
 BLK = 64
+VMEM_BYTES = 56 * 2**20
 
 
 learn_rate = 0.002
@@ -29,11 +32,99 @@
     return moved.astype(jnp.bfloat16)
 
 
-def assemble(tile_rows, row_pick, col_pick):
-    stacked = tile_rows.reshape(tile_rows.shape[0], BLK, BLK)
-    tile_grid = jnp.zeros((D // BLK, R // BLK, BLK, BLK), jnp.bfloat16)
-    tile_grid = tile_grid.at[row_pick, col_pick].set(stacked)
-    return tile_grid.transpose(0, 2, 1, 3).reshape(D, R)
+def pack_pairs(tile_rows):
+    half = tile_rows.shape[0] // 2
+    halves = tile_rows.reshape(2, half, BLK, BLK)
+    return halves.transpose(1, 2, 0, 3).reshape(half, BLK, 2 * BLK)
+
+
+def unpack_pairs(pairs):
+    half = pairs.shape[0]
+    halves = pairs.reshape(half, BLK, 2, BLK).transpose(2, 0, 1, 3)
+    return halves.reshape(2 * half, BLK * BLK)
+
+
+def swap_halves(value):
+    return jnp.concatenate([value[:, BLK:], value[:, :BLK]], axis=1)
+
+
+def lane_half():
+    return lax.broadcasted_iota(jnp.int32, (BLK, 2 * BLK), 1) // BLK
+
+
+def block_numbers(pair, half):
+    first = (pair // half) * (2 * half) + pair % half
+    return (first, first + half)
+
+
+def assemble_kernel(half, rows_ref, cols_ref, pairs_ref, out_ref):
+    @pl.loop(0, D // 512)
+    def _(chunk):
+        out_ref[pl.ds(pl.multiple_of(chunk * 512, 512), 512), :] = jnp.zeros((512, R), jnp.bfloat16)
+
+    @pl.loop(0, pairs_ref.shape[0], unroll=4)
+    def _(pair):
+        straight = pairs_ref[pair]
+        swapped = swap_halves(straight)
+        for side, number in enumerate(block_numbers(pair, half)):
+            row, col = rows_ref[number], cols_ref[number]
+            parity = col % 2
+            at = (
+                pl.ds(pl.multiple_of(row * BLK, BLK), BLK),
+                pl.ds(pl.multiple_of((col // 2) * 2 * BLK, 2 * BLK), 2 * BLK),
+            )
+            tile = jnp.where(parity == side, straight, swapped)
+            out_ref[at] = jnp.where(lane_half() == parity, tile, out_ref[at])
+
+
+def assemble(pairs, row_pick, col_pick, half):
+    return pl.pallas_call(
+        functools.partial(assemble_kernel, half),
+        out_shape=jax.ShapeDtypeStruct((D, R), jnp.bfloat16),
+        in_specs=[pl.BlockSpec(memory_space=pltpu.SMEM)] * 2
+        + [pl.BlockSpec(memory_space=pltpu.VMEM)],
+        out_specs=pl.BlockSpec(memory_space=pltpu.VMEM),
+        compiler_params=pltpu.CompilerParams(vmem_limit_bytes=VMEM_BYTES),
+        name="assemble",
+    )(row_pick, col_pick, pairs)
+
+
+def grads_kernel(half, rows_ref, cols_ref, left_ref, right_ref, out_ref, dense):
+    @pl.loop(0, D // 512)
+    def _(chunk):
+        at = pl.ds(pl.multiple_of(chunk * 512, 512), 512)
+        dense[at, :] = lax.dot_general(
+            left_ref[:, at],
+            right_ref[...],
+            (((0,), (0,)), ((), ())),
+            preferred_element_type=jnp.float32,
+        ).astype(jnp.bfloat16)
+
+    @pl.loop(0, out_ref.shape[0], unroll=4)
+    def _(pair):
+        tiles = []
+        for side, number in enumerate(block_numbers(pair, half)):
+            row, col = rows_ref[number], cols_ref[number]
+            tile = dense[
+                pl.ds(pl.multiple_of(row * BLK, BLK), BLK),
+                pl.ds(pl.multiple_of((col // 2) * 2 * BLK, 2 * BLK), 2 * BLK),
+            ]
+            tiles.append(jnp.where(col % 2 == side, tile, swap_halves(tile)))
+        out_ref[pair] = jnp.where(lane_half() == 0, tiles[0], tiles[1])
+
+
+def block_grads(left_cat, right_cat, row_pick, col_pick, half):
+    pairs = row_pick.shape[0] // 2
+    return pl.pallas_call(
+        functools.partial(grads_kernel, half),
+        out_shape=jax.ShapeDtypeStruct((pairs, BLK, 2 * BLK), jnp.bfloat16),
+        in_specs=[pl.BlockSpec(memory_space=pltpu.SMEM)] * 2
+        + [pl.BlockSpec(memory_space=pltpu.VMEM)] * 2,
+        out_specs=pl.BlockSpec(memory_space=pltpu.VMEM),
+        scratch_shapes=[pltpu.VMEM((D, R), jnp.bfloat16)],
+        compiler_params=pltpu.CompilerParams(vmem_limit_bytes=VMEM_BYTES),
+        name="block_grads",
+    )(row_pick, col_pick, left_cat, right_cat)
 
 
 def transpose_product(left_side, matrix):
@@ -42,8 +133,8 @@
     )
 
 
-def make_products(tile_flat, row_pick, col_pick):
-    matrix = assemble(tile_flat, row_pick, col_pick)
+def make_products(pairs, row_pick, col_pick, half):
+    matrix = assemble(pairs, row_pick, col_pick, half)
 
     def times_matrix(left_side):
         return jnp.dot(left_side, matrix, preferred_element_type=jnp.float32)
@@ -70,12 +161,13 @@
     micro_count, tok_rows, model_width = inputs.shape
     gain_row = norm_gain[0]
     local_blocks = extrapolate(blocks[0], first_moment[0], second_moment[0], delays[0])
-    all_blocks, all_rows, all_cols = (
-        lax.all_gather(local_blocks, "fsdp", axis=0, tiled=True),
-        lax.all_gather(row_index[0], "fsdp", axis=0, tiled=True),
-        lax.all_gather(col_index[0], "fsdp", axis=0, tiled=True),
-    )
-    forward_matrix, forward_transpose = make_products(all_blocks, all_rows, all_cols)
+    half = local_blocks.shape[0] // 2
+    all_pairs = lax.all_gather(pack_pairs(local_blocks), "fsdp", axis=0, tiled=True)
+    positions = lax.all_gather(
+        jnp.stack([row_index[0], col_index[0]]), "fsdp", axis=1, tiled=True
+    )
+    all_rows, all_cols = positions[0], positions[1]
+    forward_matrix, forward_transpose = make_products(all_pairs, all_rows, all_cols, half)
     tick_count = micro_count + phases - 1
 
     def forward_compute(tick, incoming, stores):
@@ -186,26 +278,9 @@
     right_cat = jnp.concatenate(
         [dpre_all.reshape(token_total, R), act_all.reshape(token_total, R)], axis=0
     )
-    left_tiles = left_cat.T.reshape(model_width // BLK, BLK, 2 * token_total)
-    right_tiles = right_cat.T.reshape(R // BLK, BLK, 2 * token_total)
-    row_count = local_blocks.shape[0] * lax.axis_size("fsdp")
-    group_size = math.gcd(row_count, 64)
-
-    def one_group(group_id):
-        rows_now = lax.dynamic_slice_in_dim(all_rows, group_id * group_size, group_size)
-        cols_now = lax.dynamic_slice_in_dim(all_cols, group_id * group_size, group_size)
-        left_rows = jnp.take(left_tiles, rows_now, axis=0)
-        right_rows = jnp.take(right_tiles, cols_now, axis=0)
-        product = jnp.einsum(
-            "nit,njt->nij", left_rows, right_rows, preferred_element_type=jnp.float32
-        )
-        return product.reshape(group_size, BLK * BLK)
-
-    results = lax.map(one_group, jnp.arange(row_count // group_size, dtype=jnp.int32))
-    rounded = lax.optimization_barrier(results.reshape(row_count, BLK * BLK).astype(jnp.bfloat16))
-    weight_part = lax.psum_scatter(
-        rounded.astype(jnp.float32).astype(jnp.bfloat16), "fsdp", scatter_dimension=0, tiled=True
-    ).astype(jnp.float32)
+    parts = block_grads(left_cat, right_cat, all_rows, all_cols, half)
+    weight_pairs = lax.psum_scatter(parts, "fsdp", scatter_dimension=0, tiled=True)
+    weight_part = unpack_pairs(weight_pairs.astype(jnp.float32))
     gain_part = lax.psum(gain_total.astype(jnp.bfloat16), "fsdp").astype(jnp.float32)
     return (weight_part[None], gain_part[None])
 

time: 1110 us -> 713 us (0.64)
  local copies, waits for them, and re-layouts: 404 us -> 37.2 us
  Pallas kernels: 0 us -> 58.4 us
  matrix products: 135 us -> 81.9 us
  blocking collectives: 74.5 us -> 58.5 us
  other arithmetic: 48 us -> 32.7 us
  waiting for transfers between devices: 355 us -> 370 us
  loops' own time: 11.9 us -> 0.53 us
    unnamed x23 -> x10, local copies, waits for them, and re-layouts: 151 us -> 0.72 us
    gather x32 -> x0, local copies, waits for them, and re-layouts: 77.9 us -> none  [the longest x16 67 us: one_group(): left_rows = jnp.take(left_tiles, rows_now, axis=0)]
    reshape x2 -> x1, local copies, waits for them, and re-layouts: 68.1 us -> 4.77 us  [pack_pairs(): return halves.transpose(1, 2, 0, 3).reshape(half, BLK, 2 * BLK)]
    pallas_call x0 -> x2, Pallas kernels: none -> 58.4 us  [the longest x1 32.4 us: block_grads(): pl.pallas_call(functools.partial(grads_kernel, half), out_shape=jax.Shape...]
    dot_general x16 -> x0, matrix products: 53.4 us -> none  [one_group(): jnp.einsum('nit,njt->nij', left_rows, right_rows, preferred_element_type=...]
    transpose x3 -> x0, local copies, waits for them, and re-layouts: 40.6 us -> none  [the longest x1 34 us: assemble(): return tile_grid.transpose(0, 2, 1, 3).reshape(D, R)]
    broadcast_in_dim x16 -> x0, local copies, waits for them, and re-layouts: 33 us -> none  [shards(): lax.map(one_group, jnp.arange(row_count // group_size, dtype=jnp.int32))]
    all_gather x2 -> x1, blocking collectives: 38.6 us -> 22.7 us  [shards(): lax.all_gather(jnp.stack([row_index[0], col_index[0]]), 'fsdp', axis=1, t...]
where the time goes in v1:
time: 713 us; the launch traced here: 712 us
  waiting for transfers between devices  370 us (52%)
  matrix products  81.9 us (11%)
  blocking collectives  58.5 us (8%)
  Pallas kernels  58.4 us (8%)
  starting transfers between devices  57.2 us (8%)
  local copies, waits for them, and re-layouts  37.2 us (5%)
  other arithmetic  32.7 us (5%)
  between operations  14.8 us (2%)
    ppermute x8, waiting for transfers between devices, shifted(): lax.ppermute(value, axis, [(source, source + steps) for source in range(i...  156 us
    reduce_scatter x1, waiting for transfers between devices, shards(): lax.psum_scatter(parts, 'fsdp', scatter_dimension=0, tiled=True)  110 us
    all_gather x1, waiting for transfers between devices, shards(): lax.all_gather(pack_pairs(local_blocks), 'fsdp', axis=0, tiled=True)  104 us
    ppermute x8, starting transfers between devices, shifted(): lax.ppermute(value, axis, [(source, source + steps) for source in range(i...  57.1 us
    dot_general x4, matrix products, transpose_product(): lax.dot_general(left_side, matrix, (((1,), (1,)), ((), ())), preferred_el...  44.7 us
    dot_general x4, matrix products, times_matrix(): return jnp.dot(left_side, matrix, preferred_element_type=jnp.float32)  37.2 us
    psum x1, blocking collectives, shards(): lax.psum(gain_total.astype(jnp.bfloat16), 'fsdp').astype(jnp.float32)  35.7 us
    pallas_call x1, Pallas kernels, block_grads(): pl.pallas_call(functools.partial(grads_kernel, half), out_shape=jax.Shape...  32.4 us
  transfers between devices with their start and end apart: 10, of which 10 were waited for; matrix products, arithmetic and copies ran while one was open for 0% of the time, Pallas kernels for 0%

profile of v1, /device:TPU:0, one launch (start us, length us, event | category | flops | bytes accessed | tf_op | source)
XLA Modules:
  0.0 711.6 jit_solution(17902558927998008520)
XLA Ops:
  13.6 3.5 copy.16
  17.0 4.8 reshape.101
  21.9 22.7 %all_gather.6 = s32[2,1024]{1,0:T(2,128)S(1)} all-gather(s32[2,128]{1,0:T(2,128)S(1)} %pad_add_fusion), channel_id=1, replica_groups=mesh['phase'=4,'fsdp'=8] {'fsdp'}, dimensions={1}, use_global_device_ids=true | all-gather | bytes 9216 | tf_op jit(solution)/shard_map/all_gather | solution.py:166
  45.3 104.4 %all-gather.2.cloned.1.call-done.pairs_ref = bf16[512,64,128]{2,1,0:T(8,128)(2,1)} async-done(((bf16[64,64,128]{2,1,0:T(8,128)(2,1)}), bf16[512,64,128]{2,1,0:T(8,128)(2,1)}) %all-gather.2.cloned.1.call-update) | async-done | bytes 8388624 | tf_op jit(solution)/shard_map/all_gather | solution.py:165
  149.7 26.0 %assemble.1 = bf16[8192,1024]{1,0:T(8,128)(2,1)} custom-call(s32[1024]{0:T(1024)} %bitcast.126, s32[1024]{0:T(1024)} %bitcast.124, bf16[512,64,128]{2,1,0:T(8,128)(2,1)} %all-gather.2.cloned.1.call-done.pairs_ref), custom_call_target="tpu_custom_call" | custom-call | tf_op jit(solution)/shard_map/assemble/pallas_call | solution.py:81
  179.7 112.7 %while.43 = (s32[]{:T(128)}, bf16[64,8192]{1,0:T(8,128)(2,1)S(1)}, bf16[2,64,8192]{2,1,0:T(8,128)(2,1)}, bf16[2,64,8192]{2,1,0:T(8,128)(2,1)}, f32[2,64,1024]{2,...) while((s32[]{:T(128)}, bf16[64,8192]{1,0:T(8,128)(2,1)S(1)}, ...), condition=%wide.region_4.5_spmd, body=%wide.region_0.4_spmd.sunk | while | flops 2156003328 | bytes 53675808 | solution.py:210
  181.1 23.1 %conditional.8 = (bf16[64,8192]{1,0:T(8,128)(2,1)S(1)}, bf16[2,64,8192]{2,1,0:T(8,128)(2,1)}, bf16[2,64,8192]{2,1,0:T(8,128)(2,1)}, f32[2,64,1024]{2,1,0:T(8,128)}, bf16[2,64,1024]{2,1,0:T(8,128)(2,1)S(1)}) conditional(s32[]{:T(128)} %convert_element_type.155, (bf16[64,8192]{1,0:T(8,128)(2,1)S(1)}, bf16[2,64,8192]{2,1,0:T(8,128)(2,1)}, ...), branch_computations={%region_1.1_spmd, %region_2.3_spmd} | conditional | flops 2155479040 | bytes 46335432 | solution.py:196
  181.8 9.6 %bitcast_dynamic-update-slice_fusion.2 = (f32[2,64,1024]{2,1,0:T(8,128)}, f32[64,1024]{1,0:T(8,128)S(1)}) fusion(f32[2,64,1024]{2,1,0:T(8,128)} %get-tuple-element.706, s32[]{:T(128)S(6)} %select_n.89, bf16[8192,1024]{1,0:T(8,128)(2,1)} %get-tuple-element.702, bf16[64,8192]{1,0:T(8,128)(2,1)S(1)} %get-tuple-element.700, f32[8192]{0:T(1024)S(1)} %bitcast.112, ...), kind=kOutput, calls=%fused_computation.10 | convolution fusion | flops 1075838976 | bytes 18383108 | tf_op jit(solution)/shard_map/while/body/eval_jaxpr/cond/branch_1_fun/dot_general | solution.py:140
  191.6 11.0 %fusion = bf16[64,8192]{1,0:T(8,128)(2,1)S(1)} fusion(bf16[8192,1024]{1,0:T(8,128)(2,1)} %get-tuple-element.702, bf16[64,8192]{1,0:T(8,128)(2,1)S(1)} %get-tuple-element.700, f32[64,1024]{1,0:T(8,128)S(1)} %get-tuple-element.869), kind=kOutput, calls=%fused_computation.1 | convolution fusion | flops 1075642368 | bytes 19136512 | tf_op jit(solution)/shard_map/while/body/eval_jaxpr/cond/branch_1_fun/dot_general | solution.py:131
  209.1 23.1 %conditional.8 = (bf16[64,8192]{1,0:T(8,128)(2,1)S(1)}, bf16[2,64,8192]{2,1,0:T(8,128)(2,1)}, bf16[2,64,8192]{2,1,0:T(8,128)(2,1)}, f32[2,64,1024]{2,1,0:T(8,128)}, bf16[2,64,1024]{2,1,0:T(8,128)(2,1)S(1)}) conditional(s32[]{:T(128)} %convert_element_type.155, (bf16[64,8192]{1,0:T(8,128)(2,1)S(1)}, bf16[2,64,8192]{2,1,0:T(8,128)(2,1)}, ...), branch_computations={%region_1.1_spmd, %region_2.3_spmd} | conditional | flops 2155479040 | bytes 46335432 | solution.py:196
  209.9 9.6 %bitcast_dynamic-update-slice_fusion.2 = (f32[2,64,1024]{2,1,0:T(8,128)}, f32[64,1024]{1,0:T(8,128)S(1)}) fusion(f32[2,64,1024]{2,1,0:T(8,128)} %get-tuple-element.706, s32[]{:T(128)S(6)} %select_n.89, bf16[8192,1024]{1,0:T(8,128)(2,1)} %get-tuple-element.702, bf16[64,8192]{1,0:T(8,128)(2,1)S(1)} %get-tuple-element.700, f32[8192]{0:T(1024)S(1)} %bitcast.112, ...), kind=kOutput, calls=%fused_computation.10 | convolution fusion | flops 1075838976 | bytes 18383108 | tf_op jit(solution)/shard_map/while/body/eval_jaxpr/cond/branch_1_fun/dot_general | solution.py:140
  219.6 11.0 %fusion = bf16[64,8192]{1,0:T(8,128)(2,1)S(1)} fusion(bf16[8192,1024]{1,0:T(8,128)(2,1)} %get-tuple-element.702, bf16[64,8192]{1,0:T(8,128)(2,1)S(1)} %get-tuple-element.700, f32[64,1024]{1,0:T(8,128)S(1)} %get-tuple-element.869), kind=kOutput, calls=%fused_computation.1 | convolution fusion | flops 1075642368 | bytes 19136512 | tf_op jit(solution)/shard_map/while/body/eval_jaxpr/cond/branch_1_fun/dot_general | solution.py:131
  238.2 34.5 %collective-permute-start = (bf16[64,8192]{1,0:T(8,128)(2,1)S(1)}, bf16[64,8192]{1,0:T(8,128)(2,1)S(1)}, u32[]{:S(2)}, u32[]{:S(2)}) collective-permute-start(bf16[64,8192]{1,0:T(8,128)(2,1)S(1)} %get-tuple-element.1018), channel_id=1, source_target_pairs={{0,8},{8,16},{16,24},{1,9},{9,17},{17,25},{2,10},{10,18},{18,26},{... | collective-permute-start | bytes 3145736 | tf_op jit(solution)/shard_map/while/body/eval_jaxpr/ppermute | solution.py:24
  276.4 13.9 %collective-permute-start = (bf16[64,8192]{1,0:T(8,128)(2,1)S(1)}, bf16[64,8192]{1,0:T(8,128)(2,1)S(1)}, u32[]{:S(2)}, u32[]{:S(2)}) collective-permute-start(bf16[64,8192]{1,0:T(8,128)(2,1)S(1)} %get-tuple-element.1018), channel_id=1, source_target_pairs={{0,8},{8,16},{16,24},{1,9},{9,17},{17,25},{2,10},{10,18},{18,26},{... | collective-permute-start | bytes 3145736 | tf_op jit(solution)/shard_map/while/body/eval_jaxpr/ppermute | solution.py:24
  294.8 186.3 %while.44 = (s32[]{:T(128)}, bf16[64,8192]{1,0:T(8,128)(2,1)S(1)}, bf16[2,64,8192]{2,1,0:T(8,128)(2,1)}, bf16[2,64,1024]{2,1,0:T(8,128)(2,1)S(1)}, f32[8192]{0:T...) while((s32[]{:T(128)}, bf16[64,8192]{1,0:T(8,128)(2,1)S(1)}, ...), condition=%wide.region_14.15_spmd, body=%wide.region_8.14_spmd.sunk | while | flops 2158559232 | bytes 56429296 | solution.py:263
  298.5 37.9 %collective-permute-done.1 = bf16[64,8192]{1,0:T(8,128)(2,1)S(1)} collective-permute-done((bf16[64,8192]{1,0:T(8,128)(2,1)}, bf16[64,8192]{1,0:T(8,128)(2,1)S(1)}, u32[]{:S(2)}, u32[]{:S(2)}) %collective-permute-start.1) | collective-permute-done | bytes 1048608 | tf_op jit(solution)/shard_map/while/body/eval_jaxpr/ppermute | solution.py:24
  340.0 15.8 %collective-permute-done.1 = bf16[64,8192]{1,0:T(8,128)(2,1)S(1)} collective-permute-done((bf16[64,8192]{1,0:T(8,128)(2,1)}, bf16[64,8192]{1,0:T(8,128)(2,1)S(1)}, u32[]{:S(2)}, u32[]{:S(2)}) %collective-permute-start.1) | collective-permute-done | bytes 1048608 | tf_op jit(solution)/shard_map/while/body/eval_jaxpr/ppermute | solution.py:24
  359.4 78.3 %collective-permute-done.1 = bf16[64,8192]{1,0:T(8,128)(2,1)S(1)} collective-permute-done((bf16[64,8192]{1,0:T(8,128)(2,1)}, bf16[64,8192]{1,0:T(8,128)(2,1)S(1)}, u32[]{:S(2)}, u32[]{:S(2)}) %collective-permute-start.1) | collective-permute-done | bytes 1048608 | tf_op jit(solution)/shard_map/while/body/eval_jaxpr/ppermute | solution.py:24
  439.0 25.8 %conditional.9 = (bf16[64,8192]{1,0:T(8,128)(2,1)}, bf16[2,64,8192]{2,1,0:T(8,128)(2,1)}, bf16[2,64,1024]{2,1,0:T(8,128)(2,1)S(1)}, f32[8192]{0:T(1024)S(1)}) conditional(s32[]{:T(128)} %convert_element_type.156, (bf16[64,8192]{1,0:T(8,128)(2,1)S(1)}, bf16[2,64,8192]{2,1,0:T(8,128)(2,1)}, bf16[2,64,1024]{2,1,0:T(8,128)(2,1)S(1)}, ...), branch_computations={%region_9.9_spmd, %region_10.13_spmd} | conditional | flops 2158034944 | bytes 49088912 | solution.py:250
  439.0 8.8 %bitcast_dynamic-update-slice_fusion.9 = (bf16[2,64,1024]{2,1,0:T(8,128)(2,1)S(1)}, bf16[64,1024]{1,0:T(8,128)(2,1)S(1)}) fusion(bf16[2,64,1024]{2,1,0:T(8,128)(2,1)S(1)} %get-tuple-element.742, s32[]{:T(128)S(6)} %select_n.95, f32[2,64,1024]{2,1,0:T(8,128)} %get-tuple-element.739, bf16[64,8192]{1,0:T(8,128)(2,1)S(1)} %get-tuple-element.735, ...), kind=kOutput, calls=%fused_computation.50 | convolution fusion | flops 1074331648 | bytes 18350084 | tf_op jit(solution)/shard_map/while/body/eval_jaxpr/cond/branch_1_fun/dot_general | solution.py:140
  449.5 11.4 %fusion.19 = (f32[8192]{0:T(1024)S(1)}, f32[64]{0:T(128)S(1)}, f32[64,8192]{1,0:T(8,128)S(1)}) fusion(f32[64]{0:T(128)S(1)} %add_rsqrt_fusion.2, bf16[2,64,8192]{2,1,0:T(8,128)(2,1)} %get-tuple-element.736, s32[]{:T(128)S(6)} %select_n.95, f32[8192]{0:T(1024)S(1)} %bitcast.116, bf16[64,1024]{1,0:T(8,128)(2,1)S(1)} %get-tuple-element.872, ...), kind=kOutput, calls=%fused_computation.38 | convolution fusion | flops 1077403648 | bytes 20120068 | tf_op jit(solution)/shard_map/while/body/eval_jaxpr/cond/branch_1_fun/dot_general | solution.py:131
  466.1 15.0 %collective-permute-done.1 = bf16[64,8192]{1,0:T(8,128)(2,1)S(1)} collective-permute-done((bf16[64,8192]{1,0:T(8,128)(2,1)}, bf16[64,8192]{1,0:T(8,128)(2,1)S(1)}, u32[]{:S(2)}, u32[]{:S(2)}) %collective-permute-start.1) | collective-permute-done | bytes 1048608 | tf_op jit(solution)/shard_map/while/body/eval_jaxpr/ppermute | solution.py:24
  481.2 24.3 %conditional.5 = (f32[8192]{0:T(1024)S(1)}, bf16[128,8192]{1,0:T(8,128)(2,1)}, bf16[128,1024]{1,0:T(8,128)(2,1)S(1)}) conditional(s32[]{:T(128)} %convert_element_type.97, (f32[8192]{0:T(1024)S(1)}, bf16[2,64,8192]{2,1,0:T(8,128)(2,1)}, bf16[2,64,1024]{2,1,0:T(8,128)(2,1)S(1)}) %tuple.162, (pred[]{:T(512)}, s32[]{:T(128)}, ...), branch_computations={%region_15.16_spmd, %region_16.19_spmd} | conditional | flops 2152792064 | bytes 41684028 | solution.py:250
  481.2 9.1 %bitcast_dynamic-update-slice_fusion.11 = (bf16[2,64,1024]{2,1,0:T(8,128)(2,1)S(1)}, bf16[64,1024]{1,0:T(8,128)(2,1)S(1)}) fusion(bf16[2,64,1024]{2,1,0:T(8,128)(2,1)S(1)} %get-tuple-element.770, s32[]{:T(128)S(6)} %min.25, f32[2,64,1024]{2,1,0:T(8,128)} %get-tuple-element.767, bf16[8192,1024]{1,0:T(8,128)(2,1)} %get-tuple-element.766, ...), kind=kOutput, calls=%fused_computation.70 | convolution fusion | flops 1074855936 | bytes 19400192 | tf_op jit(solution)/shard_map/cond/branch_1_fun/dot_general | solution.py:140
  491.8 11.2 %fusion.28 = f32[8192]{0:T(1024)S(1)} fusion(bf16[64,1024]{1,0:T(8,128)(2,1)S(1)} %get-tuple-element.874, bf16[8192,1024]{1,0:T(8,128)(2,1)} %get-tuple-element.766, f32[64]{0:T(128)S(1)} %add_rsqrt_fusion.3, bf16[2,64,8192]{2,1,0:T(8,128)(2,1)} %get-tuple-element.768, s32[]{:T(128)S(6)} %min.25), kind=kOutput, calls=%fused_computation.58 | convolution fusion | flops 1075830784 | bytes 17989892 | tf_op jit(solution)/shard_map/cond/branch_1_fun/dot_general | solution.py:131
  506.4 4.6 pad_maximum_fusion.left_ref
  511.0 32.4 %block_grads.1 = bf16[512,64,128]{2,1,0:T(8,128)(2,1)} custom-call(s32[1024]{0:T(1024)} %bitcast.127, s32[1024]{0:T(1024)} %bitcast.125, bf16[256,8192]{1,0:T(8,128)(2,1)} %pad_maximum_fusion.left_ref, bf16[256,1024]{1,0:T(8,128)(2,1)} %pad_maximum_fusion.1.right_ref), custom_call_target="tpu_custom_call" | custom-call | tf_op jit(solution)/shard_map/block_grads/pallas_call | solution.py:118
  543.5 35.7 %psum.7 = bf16[1,8192]{1,0:T(2,128)(2,1)S(1)} all-reduce(bf16[1,8192]{1,0:T(2,128)(2,1)S(1)} %broadcast_in_dim.70), channel_id=1, replica_groups=mesh['phase'=4,'fsdp'=8] {'fsdp'}, use_global_device_ids=true, to_apply=%region_20.21 | all-reduce | flops 8192 | bytes 32768 | tf_op jit(solution)/shard_map/psum | solution.py:284
  579.8 110.2 %reduce-scatter.2.cloned.1.call-done = bf16[64,64,128]{2,1,0:T(8,128)(2,1)} async-done(((bf16[512,64,128]{2,1,0:T(8,128)(2,1)}), bf16[64,64,128]{2,1,0:T(8,128)(2,1)}) %reduce-scatter.2.cloned.1.call-update) | async-done | bytes 1048592 | tf_op jit(solution)/shard_map/reduce_scatter | solution.py:282
  690.0 5.2 reshape.118
  695.2 4.7 copy.14
  700.0 4.8 reshape.117
  (98 shorter events, 63.2 us)
Async XLA Ops:
  7.2 142.5 %all-gather.2.cloned.1.call-start = ((), (), s32[]{:S(2)}) async-start(), calls=%async_computation.1 | async-start | bytes 9437184 | tf_op jit(solution)/shard_map/all_gather | solution.py:165
  17.0 4.9 copy-start.9
  17.0 4.9 copy-start.10
  21.8 668.1 %reduce-scatter.2.cloned.1.call-start = ((), (), s32[]{:S(2)}) async-start(), calls=%async_computation.2 | async-start | bytes 9437184 | tf_op jit(solution)/shard_map/reduce_scatter | solution.py:282
  177.2 2.5 copy-start
  181.1 0.7 copy-start.1
  181.8 9.6 %copy-start.2 = (bf16[2,64,1024]{2,1,0:T(8,128)(2,1)S(1)}, bf16[2,64,1024]{2,1,0:T(8,128)(2,1)}, u32[]{:S(2)}) copy-start(bf16[2,64,1024]{2,1,0:T(8,128)(2,1)} %copy-done.1) | copy-start | bytes 786436 | tf_op jit(solution)/shard_map/while/body/eval_jaxpr/cond
  191.5 11.0 %copy-start.3 = (bf16[2,64,1024]{2,1,0:T(8,128)(2,1)}, bf16[2,64,1024]{2,1,0:T(8,128)(2,1)S(1)}, u32[]{:S(2)}) copy-start(bf16[2,64,1024]{2,1,0:T(8,128)(2,1)S(1)} %bitcast_dynamic-update-slice_fusion.3) | copy-start | bytes 786436 | tf_op jit(solution)/shard_map/while/body/eval_jaxpr/cond
  202.6 1.6 copy-start.4
  204.2 3.6 collective-permute-start
  209.1 0.7 copy-start.1
  209.9 9.6 %copy-start.2 = (bf16[2,64,1024]{2,1,0:T(8,128)(2,1)S(1)}, bf16[2,64,1024]{2,1,0:T(8,128)(2,1)}, u32[]{:S(2)}) copy-start(bf16[2,64,1024]{2,1,0:T(8,128)(2,1)} %copy-done.1) | copy-start | bytes 786436 | tf_op jit(solution)/shard_map/while/body/eval_jaxpr/cond
  219.6 11.0 %copy-start.3 = (bf16[2,64,1024]{2,1,0:T(8,128)(2,1)}, bf16[2,64,1024]{2,1,0:T(8,128)(2,1)S(1)}, u32[]{:S(2)}) copy-start(bf16[2,64,1024]{2,1,0:T(8,128)(2,1)S(1)} %bitcast_dynamic-update-slice_fusion.3) | copy-start | bytes 786436 | tf_op jit(solution)/shard_map/while/body/eval_jaxpr/cond
  230.6 1.7 copy-start.4
  232.3 4.5 collective-permute-start
  238.2 36.7 %collective-permute-start = (bf16[64,8192]{1,0:T(8,128)(2,1)S(1)}, bf16[64,8192]{1,0:T(8,128)(2,1)S(1)}, u32[]{:S(2)}, u32[]{:S(2)}) collective-permute-start(bf16[64,8192]{1,0:T(8,128)(2,1)S(1)} %get-tuple-element.1018), channel_id=1, source_target_pairs={{0,8},{8,16},{16,24},{1,9},{9,17},{17,25},{2,10},{10,18},{18,26},{... | collective-permute-start | bytes 3145736 | tf_op jit(solution)/shard_map/while/body/eval_jaxpr/ppermute | solution.py:24
  276.4 16.1 %collective-permute-start = (bf16[64,8192]{1,0:T(8,128)(2,1)S(1)}, bf16[64,8192]{1,0:T(8,128)(2,1)S(1)}, u32[]{:S(2)}, u32[]{:S(2)}) collective-permute-start(bf16[64,8192]{1,0:T(8,128)(2,1)S(1)} %get-tuple-element.1018), channel_id=1, source_target_pairs={{0,8},{8,16},{16,24},{1,9},{9,17},{17,25},{2,10},{10,18},{18,26},{... | collective-permute-start | bytes 3145736 | tf_op jit(solution)/shard_map/while/body/eval_jaxpr/ppermute | solution.py:24
  292.5 0.7 copy-start.5
  297.2 39.2 %collective-permute-start.1 = (bf16[64,8192]{1,0:T(8,128)(2,1)}, bf16[64,8192]{1,0:T(8,128)(2,1)S(1)}, u32[]{:S(2)}, u32[]{:S(2)}) collective-permute-start(bf16[64,8192]{1,0:T(8,128)(2,1)} %get-tuple-element.1035), channel_id=1, source_target_pairs={{8,0},{16,8},{24,16},{9,1},{17,9},{25,17},{10,2},{18,10},{26,18},{... | collective-permute-start | bytes 3145736 | tf_op jit(solution)/shard_map/while/body/eval_jaxpr/ppermute | solution.py:24
  338.7 17.1 %collective-permute-start.1 = (bf16[64,8192]{1,0:T(8,128)(2,1)}, bf16[64,8192]{1,0:T(8,128)(2,1)S(1)}, u32[]{:S(2)}, u32[]{:S(2)}) collective-permute-start(bf16[64,8192]{1,0:T(8,128)(2,1)} %get-tuple-element.1035), channel_id=1, source_target_pairs={{8,0},{16,8},{24,16},{9,1},{17,9},{25,17},{10,2},{18,10},{26,18},{... | collective-permute-start | bytes 3145736 | tf_op jit(solution)/shard_map/while/body/eval_jaxpr/ppermute | solution.py:24
  358.1 79.6 %collective-permute-start.1 = (bf16[64,8192]{1,0:T(8,128)(2,1)}, bf16[64,8192]{1,0:T(8,128)(2,1)S(1)}, u32[]{:S(2)}, u32[]{:S(2)}) collective-permute-start(bf16[64,8192]{1,0:T(8,128)(2,1)} %get-tuple-element.1035), channel_id=1, source_target_pairs={{8,0},{16,8},{24,16},{9,1},{17,9},{25,17},{10,2},{18,10},{26,18},{... | collective-permute-start | bytes 3145736 | tf_op jit(solution)/shard_map/while/body/eval_jaxpr/ppermute | solution.py:24
  447.9 1.7 copy-start.7
  463.8 1.1 copy-start.8
  464.8 16.3 %collective-permute-start.1 = (bf16[64,8192]{1,0:T(8,128)(2,1)}, bf16[64,8192]{1,0:T(8,128)(2,1)S(1)}, u32[]{:S(2)}, u32[]{:S(2)}) collective-permute-start(bf16[64,8192]{1,0:T(8,128)(2,1)} %get-tuple-element.1035), channel_id=1, source_target_pairs={{8,0},{16,8},{24,16},{9,1},{17,9},{25,17},{10,2},{18,10},{26,18},{... | collective-permute-start | bytes 3145736 | tf_op jit(solution)/shard_map/while/body/eval_jaxpr/ppermute | solution.py:24
  481.2 24.3 %copy-start.6 = (bf16[128,1024]{1,0:T(8,128)(2,1)S(1)}, bf16[128,1024]{1,0:T(8,128)(2,1)}, u32[]{:S(2)}) copy-start(bf16[128,1024]{1,0:T(8,128)(2,1)} %copy-done.5) | copy-start | bytes 786436
Sparse Core Ops, SparseCore 0:
  22.0 127.6 all-gather.1
  543.5 146.4 reduce-scatter.1

commit v2 on v1

v2 whole, which is shorter than its diff:
```python
import functools

import jax
import jax.numpy as jnp
from jax import lax
from jax.experimental import pallas as pl
from jax.experimental.pallas import tpu as pltpu
from jax.sharding import PartitionSpec as P

D = 8192
R = 1024
BLK = 64
CHUNK = 1024
VMEM_BYTES = 56 * 2**20


learn_rate = 0.002
adam_epsilon = 1e-08
norm_epsilon = 1e-05


def extrapolate(tile_rows, moment_one, moment_two, delay):
    step_size = learn_rate * delay.astype(jnp.float32)
    moved = tile_rows.astype(jnp.float32) - step_size * moment_one / (
        jnp.sqrt(moment_two) + adam_epsilon
    )
    return moved.astype(jnp.bfloat16)


def pack_pairs(tile_rows):
    half = tile_rows.shape[0] // 2
    halves = tile_rows.reshape(2, half, BLK, BLK)
    return halves.transpose(1, 2, 0, 3).reshape(half, BLK, 2 * BLK)


def unpack_pairs(pairs):
    half = pairs.shape[0]
    halves = pairs.reshape(half, BLK, 2, BLK).transpose(2, 0, 1, 3)
    return halves.reshape(2 * half, BLK * BLK)


def swap_halves(value):
    return jnp.concatenate([value[:, BLK:], value[:, :BLK]], axis=1)


def lane_half():
    return lax.broadcasted_iota(jnp.int32, (BLK, 2 * BLK), 1) // BLK


def block_numbers(pair, half):
    first = (pair // half) * (2 * half) + pair % half
    return (first, first + half)


def assemble_kernel(half, rows_ref, cols_ref, pairs_ref, out_ref):
    @pl.loop(0, D // 512)
    def _(chunk):
        out_ref[pl.ds(pl.multiple_of(chunk * 512, 512), 512), :] = jnp.zeros((512, R), jnp.bfloat16)

    @pl.loop(0, pairs_ref.shape[0], unroll=4)
    def _(pair):
        straight = pairs_ref[pair]
        swapped = swap_halves(straight)
        for side, number in enumerate(block_numbers(pair, half)):
            row, col = rows_ref[number], cols_ref[number]
            parity = col % 2
            at = (
                pl.ds(pl.multiple_of(row * BLK, BLK), BLK),
                pl.ds(pl.multiple_of((col // 2) * 2 * BLK, 2 * BLK), 2 * BLK),
            )
            tile = jnp.where(parity == side, straight, swapped)
            out_ref[at] = jnp.where(lane_half() == parity, tile, out_ref[at])


def assemble(pairs, row_pick, col_pick, half):
    return pl.pallas_call(
        functools.partial(assemble_kernel, half),
        out_shape=jax.ShapeDtypeStruct((D, R), jnp.bfloat16),
        in_specs=[pl.BlockSpec(memory_space=pltpu.SMEM)] * 2
        + [pl.BlockSpec(memory_space=pltpu.VMEM)],
        out_specs=pl.BlockSpec(memory_space=pltpu.VMEM),
        compiler_params=pltpu.CompilerParams(vmem_limit_bytes=VMEM_BYTES),
        name="assemble",
    )(row_pick, col_pick, pairs)


def grads_kernel(half, rows_ref, cols_ref, left_ref, right_ref, out_ref, dense):
    @pl.loop(0, D // 512)
    def _(chunk):
        at = pl.ds(pl.multiple_of(chunk * 512, 512), 512)
        dense[at, :] = lax.dot_general(
            left_ref[:, at],
            right_ref[...],
            (((0,), (0,)), ((), ())),
            preferred_element_type=jnp.float32,
        ).astype(jnp.bfloat16)

    @pl.loop(0, out_ref.shape[0], unroll=4)
    def _(pair):
        tiles = []
        for side, number in enumerate(block_numbers(pair, half)):
            row, col = rows_ref[number], cols_ref[number]
            tile = dense[
                pl.ds(pl.multiple_of(row * BLK, BLK), BLK),
                pl.ds(pl.multiple_of((col // 2) * 2 * BLK, 2 * BLK), 2 * BLK),
            ]
            tiles.append(jnp.where(col % 2 == side, tile, swap_halves(tile)))
        out_ref[pair] = jnp.where(lane_half() == 0, tiles[0], tiles[1])


def block_grads(left_cat, right_cat, row_pick, col_pick, half):
    pairs = row_pick.shape[0] // 2
    return pl.pallas_call(
        functools.partial(grads_kernel, half),
        out_shape=jax.ShapeDtypeStruct((pairs, BLK, 2 * BLK), jnp.bfloat16),
        in_specs=[pl.BlockSpec(memory_space=pltpu.SMEM)] * 2
        + [pl.BlockSpec(memory_space=pltpu.VMEM)] * 2,
        out_specs=pl.BlockSpec(memory_space=pltpu.VMEM),
        scratch_shapes=[pltpu.VMEM((D, R), jnp.bfloat16)],
        compiler_params=pltpu.CompilerParams(vmem_limit_bytes=VMEM_BYTES),
        name="block_grads",
    )(row_pick, col_pick, left_cat, right_cat)


def relay_kernel(
    phases,
    inputs_ref,
    cotangent_ref,
    gain_ref,
    matrix_ref,
    left_ref,
    right_ref,
    total_ref,
    x_in,
    x_out,
    grad_back,
    pre_all,
    scale_all,
    sums,
    square,
    send_sem,
    recv_sem,
):
    micro_count, tok_rows, width = inputs_ref.shape
    chunks = width // CHUNK
    phase_id = lax.axis_index("phase")
    has_next, has_prev = (phase_id < phases - 1, phase_id > 0)
    after, before = (lax.rem(phase_id + 1, phases), lax.rem(phase_id + phases - 1, phases))
    barrier = pltpu.get_barrier_semaphore()

    for neighbour in (after, before):
        pl.semaphore_signal(
            barrier, inc=1, device_id={"phase": neighbour}, device_id_type=pl.DeviceIdType.MESH
        )

    def span(chunk):
        return pl.ds(pl.multiple_of(chunk * CHUNK, CHUNK), CHUNK)

    def grad_rows(batch):
        return pl.ds((micro_count + batch) * tok_rows, tok_rows)

    def batch_rows(batch):
        return pl.ds(batch * tok_rows, tok_rows)

    def forward_copy(batch, chunk):
        return pltpu.make_async_remote_copy(
            src_ref=x_out.at[batch, :, span(chunk)],
            dst_ref=x_in.at[batch, :, span(chunk)],
            send_sem=send_sem.at[0, batch, chunk],
            recv_sem=recv_sem.at[0, batch, chunk],
            device_id={"phase": after},
            device_id_type=pl.DeviceIdType.MESH,
        )

    def backward_copy(batch, chunk):
        return pltpu.make_async_remote_copy(
            src_ref=x_out.at[micro_count + batch, :, span(chunk)],
            dst_ref=grad_back.at[batch, :, span(chunk)],
            send_sem=send_sem.at[1, batch, chunk],
            recv_sem=recv_sem.at[1, batch, chunk],
            device_id={"phase": before},
            device_id_type=pl.DeviceIdType.MESH,
        )

    @pl.when(jnp.logical_not(has_prev))
    def _():
        x_in[...] = inputs_ref[...]

    @pl.when(jnp.logical_not(has_next))
    def _():
        grad_back[...] = cotangent_ref[...]

    pl.semaphore_wait(barrier, 2)

    for batch in range(micro_count):
        sums[...] = jnp.zeros_like(sums)
        square[...] = jnp.zeros_like(square)

        @pl.loop(0, chunks)
        def _(chunk):
            @pl.when(has_prev)
            def _():
                forward_copy(batch, chunk).wait_recv()

            at = span(chunk)
            x_float = x_in[batch, :, at].astype(jnp.float32)
            weighted = (x_float * gain_ref[:, at]).astype(jnp.bfloat16)
            square[...] += jnp.sum(x_float * x_float, axis=-1, keepdims=True)
            sums[...] += jnp.dot(weighted, matrix_ref[at, :], preferred_element_type=jnp.float32)

        rms_scale = lax.rsqrt(square[...] / width + norm_epsilon)
        pre = sums[...] * rms_scale
        act = (pre / (1.0 + jnp.exp(-pre))).astype(jnp.bfloat16)
        scale_all[batch] = rms_scale
        pre_all[batch] = pre
        right_ref[grad_rows(batch), :] = act

        @pl.when(has_next)
        def _():
            @pl.loop(0, chunks)
            def _(chunk):
                at = span(chunk)
                moved = transpose_product(right_ref[grad_rows(batch), :], matrix_ref[at, :])
                x_out[batch, :, at] = (x_in[batch, :, at].astype(jnp.float32) + moved).astype(
                    jnp.bfloat16
                )
                forward_copy(batch, chunk).start()

    for batch in range(micro_count):
        sums[...] = jnp.zeros_like(sums)

        @pl.loop(0, chunks)
        def _(chunk):
            @pl.when(has_next)
            def _():
                backward_copy(batch, chunk).wait_recv()

            at = span(chunk)
            sums[...] += jnp.dot(
                grad_back[batch, :, at], matrix_ref[at, :], preferred_element_type=jnp.float32
            )

        pre = pre_all[batch]
        sigmoid_pre = 1.0 / (1.0 + jnp.exp(-pre))
        dpre = (sums[...] * sigmoid_pre * (1.0 + pre * (1.0 - sigmoid_pre))).astype(jnp.bfloat16)
        right_ref[batch_rows(batch), :] = dpre
        inner = jnp.sum(dpre.astype(jnp.float32) * pre, axis=-1, keepdims=True) / width
        square[...] = inner

        @pl.loop(0, chunks)
        def _(chunk):
            at = span(chunk)
            dhidden = transpose_product(right_ref[batch_rows(batch), :], matrix_ref[at, :])
            gain_row = gain_ref[:, at]
            rms_scale = scale_all[batch]
            normed = x_in[batch, :, at].astype(jnp.float32) * rms_scale
            grad_out = grad_back[batch, :, at]
            x_out[micro_count + batch, :, at] = (
                grad_out.astype(jnp.float32)
                + rms_scale * (dhidden * gain_row - normed * square[...])
            ).astype(jnp.bfloat16)

            @pl.when(has_prev)
            def _():
                backward_copy(batch, chunk).start()

            gain_part = jnp.sum(dhidden * normed, axis=0, keepdims=True)
            if batch == 0:
                total_ref[:, at] = gain_part
            else:
                total_ref[:, at] += gain_part
            left_ref[batch_rows(batch), at] = (normed * gain_row).astype(jnp.bfloat16)
            left_ref[grad_rows(batch), at] = grad_out

    @pl.loop(0, chunks)
    def _(chunk):
        for batch in range(micro_count):
            @pl.when(has_next)
            def _():
                forward_copy(batch, chunk).wait_send()

            @pl.when(has_prev)
            def _():
                backward_copy(batch, chunk).wait_send()


def relay(inputs, cotangent, norm_gain, matrix):
    micro_count, tok_rows, width = inputs.shape
    inner = matrix.shape[1]
    vmem = pl.BlockSpec(memory_space=pltpu.VMEM)
    rows = 2 * micro_count * tok_rows
    return pl.pallas_call(
        functools.partial(relay_kernel, lax.axis_size("phase")),
        out_shape=(
            jax.ShapeDtypeStruct((rows, width), jnp.bfloat16),
            jax.ShapeDtypeStruct((rows, inner), jnp.bfloat16),
            jax.ShapeDtypeStruct((1, width), jnp.float32),
        ),
        in_specs=[vmem] * 4,
        out_specs=(vmem,) * 3,
        scratch_shapes=[
            pltpu.VMEM((micro_count, tok_rows, width), jnp.bfloat16),
            pltpu.VMEM((2 * micro_count, tok_rows, width), jnp.bfloat16),
            pltpu.VMEM((micro_count, tok_rows, width), jnp.bfloat16),
            pltpu.VMEM((micro_count, tok_rows, inner), jnp.float32),
            pltpu.VMEM((micro_count, tok_rows, 1), jnp.float32),
            pltpu.VMEM((tok_rows, inner), jnp.float32),
            pltpu.VMEM((tok_rows, 1), jnp.float32),
            pltpu.SemaphoreType.DMA((2, micro_count, width // CHUNK)),
            pltpu.SemaphoreType.DMA((2, micro_count, width // CHUNK)),
        ],
        compiler_params=pltpu.CompilerParams(
            vmem_limit_bytes=VMEM_BYTES, collective_id=0, has_side_effects=True
        ),
        name="relay",
    )(inputs, cotangent, norm_gain, matrix)


def transpose_product(left_side, matrix):
    return lax.dot_general(
        left_side, matrix, (((1,), (1,)), ((), ())), preferred_element_type=jnp.float32
    )


def shards(
    inputs, cotangent, norm_gain, blocks, first_moment, second_moment, row_index, col_index, delays
):
    local_blocks = extrapolate(blocks[0], first_moment[0], second_moment[0], delays[0])
    half = local_blocks.shape[0] // 2
    all_pairs = lax.all_gather(pack_pairs(local_blocks), "fsdp", axis=0, tiled=True)
    positions = lax.all_gather(
        jnp.stack([row_index[0], col_index[0]]), "fsdp", axis=1, tiled=True
    )
    all_rows, all_cols = positions[0], positions[1]
    matrix = assemble(all_pairs, all_rows, all_cols, half)
    left_cat, right_cat, gain_total = relay(inputs, cotangent, norm_gain, matrix)
    parts = block_grads(left_cat, right_cat, all_rows, all_cols, half)
    weight_pairs = lax.psum_scatter(parts, "fsdp", scatter_dimension=0, tiled=True)
    weight_part = unpack_pairs(weight_pairs.astype(jnp.float32))
    gain_part = lax.psum(gain_total[0].astype(jnp.bfloat16), "fsdp").astype(jnp.float32)
    return (weight_part[None], gain_part[None])


def solution(mesh):
    in_specs = (
        P(None, "fsdp", None),
        P(None, "fsdp", None),
        P("phase", None),
        P("phase", "fsdp", None),
        P("phase", "fsdp", None),
        P("phase", "fsdp", None),
        P("phase", "fsdp"),
        P("phase", "fsdp"),
        P("phase"),
    )
    out_specs = (P("phase", "fsdp", None), P("phase", None))
    return jax.shard_map(shards, mesh=mesh, in_specs=in_specs, out_specs=out_specs, check_vma=False)
```

time: 713 us -> 487 us (0.68)
  waiting for transfers between devices: 370 us -> 213 us
  Pallas kernels: 58.4 us -> 168 us
  matrix products: 81.9 us -> 0 us
  starting transfers between devices: 57.2 us -> 0.08 us
  other arithmetic: 32.7 us -> 4.09 us
  local copies, waits for them, and re-layouts: 37.2 us -> 26.6 us
    ppermute x8 -> x0, waiting for transfers between devices: 156 us -> none  [shifted(): lax.ppermute(value, axis, [(source, source + steps) for source in range(i...]
    pallas_call x0 -> x1, Pallas kernels: none -> 110 us  [relay(): pl.pallas_call(functools.partial(relay_kernel, lax.axis_size('phase')), o...]
    dot_general x8 -> x0, matrix products: 81.9 us -> none  [the longest x4 44.7 us: transpose_product(): lax.dot_general(left_side, matrix, (((1,), (1,)), ((), ())), preferred_el...]
    ppermute x8 -> x0, starting transfers between devices: 57.1 us -> none  [shifted(): lax.ppermute(value, axis, [(source, source + steps) for source in range(i...]
    select_n x8 -> x0, other arithmetic: 10.7 us -> none  [the longest x4 5.35 us: forward_compute(): phase_in = jnp.where(phase_id == 0, first_input, incoming)]
  transfers between devices with their start and end apart: 10 -> 2, of which waited for: 10 -> 2; matrix products, arithmetic and copies ran while one was open for 0% -> 0% of each run, Pallas kernels for 0% -> 0%
where the time goes in v2:
time: 487 us
  waiting for transfers between devices  213 us (44%)
  Pallas kernels  168 us (34%)
  blocking collectives  59.4 us (12%)
  local copies, waits for them, and re-layouts  26.6 us (5%)
  between operations  14.7 us (3%)
    pallas_call x1, Pallas kernels, relay(): pl.pallas_call(functools.partial(relay_kernel, lax.axis_size('phase')), o...  110 us
    reduce_scatter x1, waiting for transfers between devices, shards(): lax.psum_scatter(parts, 'fsdp', scatter_dimension=0, tiled=True)  109 us
    all_gather x1, waiting for transfers between devices, shards(): lax.all_gather(pack_pairs(local_blocks), 'fsdp', axis=0, tiled=True)  105 us
    psum x1, blocking collectives, shards(): lax.psum(gain_total[0].astype(jnp.bfloat16), 'fsdp').astype(jnp.float32)  36.9 us
    pallas_call x1, Pallas kernels, block_grads(): pl.pallas_call(functools.partial(grads_kernel, half), out_shape=jax.Shape...  32.4 us
    pallas_call x1, Pallas kernels, assemble(): pl.pallas_call(functools.partial(assemble_kernel, half), out_shape=jax.Sh...  26 us
    all_gather x1, blocking collectives, shards(): lax.all_gather(jnp.stack([row_index[0], col_index[0]]), 'fsdp', axis=1, t...  22.5 us
    another operation x3, local copies, waits for them, and re-layouts, shards(): return (weight_part[None], gain_part[None])  14.7 us
  transfers between devices with their start and end apart: 2, of which 2 were waited for; matrix products, arithmetic and copies ran while one was open for 0% of the time, Pallas kernels for 0%

profile of v2, /device:TPU:0, one launch (start us, length us, event | category | flops | bytes accessed | tf_op | source)
XLA Modules:
  0.0 486.5 jit_solution(14870983678066891444)
XLA Ops:
  7.2 0.0 all-gather.2.cloned.1.call-start
  7.9 3.4 subtract_convert_fusion
  11.3 2.3 sub.8
  13.6 3.5 copy.16
  17.0 0.0 copy-start.1
  17.0 0.0 copy-start.2
  17.0 4.8 reshape.28
  21.8 0.0 all-gather.2.cloned.1.call-update
  21.8 0.0 reduce-scatter.2.cloned.1.call-start
  21.9 0.0 copy-done.1
  21.9 0.0 copy-done.2
  21.9 22.5 %all_gather.6 = s32[2,1024]{1,0:T(2,128)S(1)} all-gather(s32[2,128]{1,0:T(2,128)S(1)} %pad_add_fusion), channel_id=1, replica_groups=mesh['phase'=4,'fsdp'=8] {'fsdp'}, dimensions={1}, use_global_device_ids=true | all-gather | bytes 9216 | tf_op jit(solution)/shard_map/all_gather | solution.py:331
  44.4 0.6 fusion
  45.0 104.6 %all-gather.2.cloned.1.call-done.pairs_ref = bf16[512,64,128]{2,1,0:T(8,128)(2,1)} async-done(((bf16[64,64,128]{2,1,0:T(8,128)(2,1)}), bf16[512,64,128]{2,1,0:T(8,128)(2,1)}) %all-gather.2.cloned.1.call-update) | async-done | bytes 8388624 | tf_op jit(solution)/shard_map/all_gather | solution.py:330
  149.6 26.0 %assemble.1.matrix_ref = bf16[8192,1024]{1,0:T(8,128)(2,1)} custom-call(s32[1024]{0:T(1024)} %bitcast.13, s32[1024]{0:T(1024)} %bitcast.11, bf16[512,64,128]{2,1,0:T(8,128)(2,1)} %all-gather.2.cloned.1.call-done.pairs_ref), custom_call_target="tpu_custom_call" | custom-call | tf_op jit(solution)/shard_map/assemble/pallas_call | solution.py:76
  175.6 109.8 %relay.1 = (bf16[256,8192]{1,0:T(8,128)(2,1)}, bf16[256,1024]{1,0:T(8,128)(2,1)}, f32[1,8192]{1,0:T(1,128)}) custom-call(bf16[2,64,8192]{2,1,0:T(8,128)(2,1)} %inputs_ref.1, bf16[2,64,8192]{2,1,0:T(8,128)(2,1)} %cotangent_ref.1, f32[1,8192]{1,0:T(1,128)} %gain_ref.1, bf16[8192,1024]{1,0:T(8,128)(2,1)} %assemble.1.matrix_ref), custom_call_target="tpu_custom_call" | custom-call | tf_op jit(solution)/shard_map/relay/pallas_call | solution.py:292
  285.5 32.4 %block_grads.1 = bf16[512,64,128]{2,1,0:T(8,128)(2,1)} custom-call(s32[1024]{0:T(1024)} %bitcast.14, s32[1024]{0:T(1024)} %bitcast.12, bf16[256,8192]{1,0:T(8,128)(2,1)} %get-tuple-element.5.left_ref, bf16[256,1024]{1,0:T(8,128)(2,1)} %get-tuple-element.6.right_ref), custom_call_target="tpu_custom_call" | custom-call | tf_op jit(solution)/shard_map/block_grads/pallas_call | solution.py:113
  317.9 0.0 copy-start
  317.9 0.0 reduce-scatter.2.cloned.1.call-update
  317.9 0.7 copy-done
  318.7 36.9 %psum.7 = bf16[1,8192]{1,0:T(2,128)(2,1)S(1)} all-reduce(bf16[1,8192]{1,0:T(2,128)(2,1)S(1)} %convert_element_type.21), channel_id=1, replica_groups=mesh['phase'=4,'fsdp'=8] {'fsdp'}, use_global_device_ids=true, to_apply=%region_1.0 | all-reduce | flops 8192 | bytes 32768 | tf_op jit(solution)/shard_map/psum | solution.py:340
  355.6 0.6 broadcast_in_dim.7
  356.2 108.7 %reduce-scatter.2.cloned.1.call-done = bf16[64,64,128]{2,1,0:T(8,128)(2,1)} async-done(((bf16[512,64,128]{2,1,0:T(8,128)(2,1)}), bf16[64,64,128]{2,1,0:T(8,128)(2,1)}) %reduce-scatter.2.cloned.1.call-update) | async-done | bytes 1048592 | tf_op jit(solution)/shard_map/reduce_scatter | solution.py:338
  465.0 5.2 %reshape.32 = f32[64,64,2,64]{3,2,1,0:T(2,128)} reshape(bf16[64,64,128]{2,1,0:T(8,128)(2,1)} %reduce-scatter.2.cloned.1.call-done) | data formatting | bytes 3145728 | tf_op jit(solution)/shard_map/broadcast_in_dim;reshape | solution.py:341
  470.2 4.8 copy.14
  474.9 4.8 reshape.31
  (2 shorter events, 0.0 us)
Async XLA Ops:
  7.2 142.5 %all-gather.2.cloned.1.call-start = ((), (), s32[]{:S(2)}) async-start(), calls=%async_computation.1 | async-start | bytes 9437184 | tf_op jit(solution)/shard_map/all_gather | solution.py:330
  17.0 4.8 copy-start.1
  17.0 4.8 copy-start.2
  21.8 443.1 %reduce-scatter.2.cloned.1.call-start = ((), (), s32[]{:S(2)}) async-start(), calls=%async_computation.2 | async-start | bytes 9437184 | tf_op jit(solution)/shard_map/reduce_scatter | solution.py:338
  317.9 0.8 copy-start
Sparse Core Ops, SparseCore 0:
  22.0 127.6 all-gather.1
  318.0 146.8 reduce-scatter.1

commit v3 on v2

--- a/solution.py
+++ b/solution.py
@@ -19,24 +19,60 @@
 norm_epsilon = 1e-05
 
 
-def extrapolate(tile_rows, moment_one, moment_two, delay):
-    step_size = learn_rate * delay.astype(jnp.float32)
-    moved = tile_rows.astype(jnp.float32) - step_size * moment_one / (
-        jnp.sqrt(moment_two) + adam_epsilon
-    )
-    return moved.astype(jnp.bfloat16)
-
-
-def pack_pairs(tile_rows):
+def lane_join(low, high):
+    return jnp.concatenate([low, high], axis=1)
+
+
+def pack_kernel(delay_ref, tiles_ref, one_ref, two_ref, out_ref, wide):
+    half = tiles_ref.shape[0] // 2
+    step_size = learn_rate * delay_ref[0].astype(jnp.float32)
+    for step in range(BLK // 2):
+        at = slice(step * 2 * BLK, (step + 1) * 2 * BLK)
+        moved = tiles_ref[:, at].astype(jnp.float32) - step_size * one_ref[:, at] / (
+            jnp.sqrt(two_ref[:, at]) + adam_epsilon
+        )
+        low, high = moved[:half], moved[half:]
+        wide[:, 2 * step, :] = lane_join(low[:, :BLK], high[:, :BLK])
+        wide[:, 2 * step + 1, :] = lane_join(low[:, BLK:], high[:, BLK:])
+    out_ref[...] = wide[...].astype(jnp.bfloat16)
+
+
+def pack_pairs(tile_rows, moment_one, moment_two, delay):
     half = tile_rows.shape[0] // 2
-    halves = tile_rows.reshape(2, half, BLK, BLK)
-    return halves.transpose(1, 2, 0, 3).reshape(half, BLK, 2 * BLK)
+    vmem = pl.BlockSpec(memory_space=pltpu.VMEM)
+    return pl.pallas_call(
+        pack_kernel,
+        out_shape=jax.ShapeDtypeStruct((half, BLK, 2 * BLK), jnp.bfloat16),
+        in_specs=[pl.BlockSpec(memory_space=pltpu.SMEM)] + [vmem] * 3,
+        out_specs=vmem,
+        scratch_shapes=[pltpu.VMEM((half, BLK, 2 * BLK), jnp.float32)],
+        compiler_params=pltpu.CompilerParams(vmem_limit_bytes=VMEM_BYTES),
+        name="pack",
+    )(delay, tile_rows, moment_one, moment_two)
+
+
+def unpack_kernel(pairs_ref, out_ref, wide):
+    half = pairs_ref.shape[0]
+    wide[...] = pairs_ref[...].astype(jnp.float32)
+    for step in range(BLK // 2):
+        at = slice(step * 2 * BLK, (step + 1) * 2 * BLK)
+        even, odd = wide[:, 2 * step, :], wide[:, 2 * step + 1, :]
+        out_ref[:half, at] = lane_join(even[:, :BLK], odd[:, :BLK])
+        out_ref[half:, at] = lane_join(even[:, BLK:], odd[:, BLK:])
 
 
 def unpack_pairs(pairs):
     half = pairs.shape[0]
-    halves = pairs.reshape(half, BLK, 2, BLK).transpose(2, 0, 1, 3)
-    return halves.reshape(2 * half, BLK * BLK)
+    vmem = pl.BlockSpec(memory_space=pltpu.VMEM)
+    return pl.pallas_call(
+        unpack_kernel,
+        out_shape=jax.ShapeDtypeStruct((2 * half, BLK * BLK), jnp.float32),
+        in_specs=[vmem],
+        out_specs=vmem,
+        scratch_shapes=[pltpu.VMEM((half, BLK, 2 * BLK), jnp.float32)],
+        compiler_params=pltpu.CompilerParams(vmem_limit_bytes=VMEM_BYTES),
+        name="unpack",
+    )(pairs)
 
 
 def swap_halves(value):
@@ -325,9 +361,9 @@
 def shards(
     inputs, cotangent, norm_gain, blocks, first_moment, second_moment, row_index, col_index, delays
 ):
-    local_blocks = extrapolate(blocks[0], first_moment[0], second_moment[0], delays[0])
-    half = local_blocks.shape[0] // 2
-    all_pairs = lax.all_gather(pack_pairs(local_blocks), "fsdp", axis=0, tiled=True)
+    half = blocks.shape[1] // 2
+    local_pairs = pack_pairs(blocks[0], first_moment[0], second_moment[0], delays)
+    all_pairs = lax.all_gather(local_pairs, "fsdp", axis=0, tiled=True)
     positions = lax.all_gather(
         jnp.stack([row_index[0], col_index[0]]), "fsdp", axis=1, tiled=True
     )
@@ -336,7 +372,7 @@
     left_cat, right_cat, gain_total = relay(inputs, cotangent, norm_gain, matrix)
     parts = block_grads(left_cat, right_cat, all_rows, all_cols, half)
     weight_pairs = lax.psum_scatter(parts, "fsdp", scatter_dimension=0, tiled=True)
-    weight_part = unpack_pairs(weight_pairs.astype(jnp.float32))
+    weight_part = unpack_pairs(weight_pairs)
     gain_part = lax.psum(gain_total[0].astype(jnp.bfloat16), "fsdp").astype(jnp.float32)
     return (weight_part[None], gain_part[None])
 

time: 487 us -> 469 us (0.963)
  local copies, waits for them, and re-layouts: 26.6 us -> 1.35 us
  Pallas kernels: 168 us -> 179 us
    another operation x3 -> x0, local copies, waits for them, and re-layouts: 14.7 us -> none  [shards(): return (weight_part[None], gain_part[None])]
    pallas_call x0 -> x2, Pallas kernels: none -> 10.9 us  [the longest x1 6.34 us: pack_pairs(): pl.pallas_call(pack_kernel, out_shape=jax.ShapeDtypeStruct((half, BLK, 2...]
    sub x2 -> x0, local copies, waits for them, and re-layouts: 5.77 us -> none  [extrapolate(): tile_rows.astype(jnp.float32)]
where the time goes in v3:
time: 469 us
  waiting for transfers between devices  213 us (45%)
  Pallas kernels  179 us (38%)
  blocking collectives  59.5 us (13%)
  between operations  14.7 us (3%)
    pallas_call x1, Pallas kernels, relay(): pl.pallas_call(functools.partial(relay_kernel, lax.axis_size('phase')), o...  110 us
    reduce_scatter x1, waiting for transfers between devices, shards(): lax.psum_scatter(parts, 'fsdp', scatter_dimension=0, tiled=True)  109 us
    all_gather x1, waiting for transfers between devices, shards(): all_pairs = lax.all_gather(local_pairs, 'fsdp', axis=0, tiled=True)  105 us
    psum x1, blocking collectives, shards(): lax.psum(gain_total[0].astype(jnp.bfloat16), 'fsdp').astype(jnp.float32)  37 us
    pallas_call x1, Pallas kernels, block_grads(): pl.pallas_call(functools.partial(grads_kernel, half), out_shape=jax.Shape...  32.4 us
    pallas_call x1, Pallas kernels, assemble(): pl.pallas_call(functools.partial(assemble_kernel, half), out_shape=jax.Sh...  26 us
    all_gather x1, blocking collectives, shards(): lax.all_gather(jnp.stack([row_index[0], col_index[0]]), 'fsdp', axis=1, t...  22.5 us
  transfers between devices with their start and end apart: 2, of which 2 were waited for; matrix products, arithmetic and copies ran while one was open for 0% of the time, Pallas kernels for 0%

profile of v3, /device:TPU:0, one launch (start us, length us, event | category | flops | bytes accessed | tf_op | source)
XLA Modules:
  0.0 468.8 jit_solution(3151681245356066075)
XLA Ops:
  7.2 0.0 all-gather.2.cloned.1.call-start
  7.9 0.0 copy-start.1
  7.9 0.0 copy-start.2
  7.9 6.3 %pack.1 = bf16[64,64,128]{2,1,0:T(8,128)(2,1)} custom-call(s32[1]{0:T(128)S(6)} %copy.11.delay_ref, bf16[128,4096]{1,0:T(8,128)(2,1)} %bitcast.9, f32[128,4096]{1,0:T(8,128)} %bitcast.6, f32[128,4096]{1,0:T(8,128)} %bitcast.7), custom_call_target="tpu_custom_call" | custom-call | tf_op jit(solution)/shard_map/pack/pallas_call | solution.py:43
  14.2 0.0 all-gather.2.cloned.1.call-update
  14.2 0.0 reduce-scatter.2.cloned.1.call-start
  14.3 0.0 copy-done.1
  14.3 0.0 copy-done.2
  14.3 22.5 %all_gather.6 = s32[2,1024]{1,0:T(2,128)S(1)} all-gather(s32[2,128]{1,0:T(2,128)S(1)} %pad_add_fusion), channel_id=1, replica_groups=mesh['phase'=4,'fsdp'=8] {'fsdp'}, dimensions={1}, use_global_device_ids=true | all-gather | bytes 9216 | tf_op jit(solution)/shard_map/all_gather | solution.py:367
  36.8 0.6 fusion
  37.4 104.6 %all-gather.2.cloned.1.call-done.pairs_ref = bf16[512,64,128]{2,1,0:T(8,128)(2,1)} async-done(((bf16[64,64,128]{2,1,0:T(8,128)(2,1)}), bf16[512,64,128]{2,1,0:T(8,128)(2,1)}) %all-gather.2.cloned.1.call-update) | async-done | bytes 8388624 | tf_op jit(solution)/shard_map/all_gather | solution.py:366
  142.0 26.0 %assemble.1.matrix_ref = bf16[8192,1024]{1,0:T(8,128)(2,1)} custom-call(s32[1024]{0:T(1024)} %bitcast.12, s32[1024]{0:T(1024)} %bitcast.10, bf16[512,64,128]{2,1,0:T(8,128)(2,1)} %all-gather.2.cloned.1.call-done.pairs_ref), custom_call_target="tpu_custom_call" | custom-call | tf_op jit(solution)/shard_map/assemble/pallas_call | solution.py:112
  168.0 109.8 %relay.1 = (bf16[256,8192]{1,0:T(8,128)(2,1)}, bf16[256,1024]{1,0:T(8,128)(2,1)}, f32[1,8192]{1,0:T(1,128)}) custom-call(bf16[2,64,8192]{2,1,0:T(8,128)(2,1)} %inputs_ref.1, bf16[2,64,8192]{2,1,0:T(8,128)(2,1)} %cotangent_ref.1, f32[1,8192]{1,0:T(1,128)} %gain_ref.1, bf16[8192,1024]{1,0:T(8,128)(2,1)} %assemble.1.matrix_ref), custom_call_target="tpu_custom_call" | custom-call | tf_op jit(solution)/shard_map/relay/pallas_call | solution.py:328
  277.9 32.4 %block_grads.1 = bf16[512,64,128]{2,1,0:T(8,128)(2,1)} custom-call(s32[1024]{0:T(1024)} %bitcast.13, s32[1024]{0:T(1024)} %bitcast.11, bf16[256,8192]{1,0:T(8,128)(2,1)} %get-tuple-element.5.left_ref, bf16[256,1024]{1,0:T(8,128)(2,1)} %get-tuple-element.6.right_ref), custom_call_target="tpu_custom_call" | custom-call | tf_op jit(solution)/shard_map/block_grads/pallas_call | solution.py:149
  310.3 0.0 copy-start
  310.3 0.0 reduce-scatter.2.cloned.1.call-update
  310.3 0.7 copy-done
  311.1 37.0 %psum.7 = bf16[1,8192]{1,0:T(2,128)(2,1)S(1)} all-reduce(bf16[1,8192]{1,0:T(2,128)(2,1)S(1)} %convert_element_type.7), channel_id=1, replica_groups=mesh['phase'=4,'fsdp'=8] {'fsdp'}, use_global_device_ids=true, to_apply=%region_1.0 | all-reduce | flops 8192 | bytes 32768 | tf_op jit(solution)/shard_map/psum | solution.py:376
  348.1 0.6 broadcast_in_dim.11
  348.8 108.6 %reduce-scatter.2.cloned.1.call-done.pairs_ref = bf16[64,64,128]{2,1,0:T(8,128)(2,1)} async-done(((bf16[512,64,128]{2,1,0:T(8,128)(2,1)}), bf16[64,64,128]{2,1,0:T(8,128)(2,1)}) %reduce-scatter.2.cloned.1.call-update) | async-done | bytes 1048592 | tf_op jit(solution)/shard_map/reduce_scatter | solution.py:374
  457.4 4.6 unpack.1
  (2 shorter events, 0.0 us)
Async XLA Ops:
  7.2 134.9 %all-gather.2.cloned.1.call-start = ((), (), s32[]{:S(2)}) async-start(), calls=%async_computation.1 | async-start | bytes 9437184 | tf_op jit(solution)/shard_map/all_gather | solution.py:366
  7.9 6.4 %copy-start.1 = (s32[1,128]{1,0:T(1,128)S(1)}, s32[1,128]{1,0:T(1,128)}, u32[]{:S(2)}) copy-start(s32[1,128]{1,0:T(1,128)} %param.16) | copy-start | bytes 1540
  7.9 6.4 %copy-start.2 = (s32[1,128]{1,0:T(1,128)S(1)}, s32[1,128]{1,0:T(1,128)}, u32[]{:S(2)}) copy-start(s32[1,128]{1,0:T(1,128)} %param.15) | copy-start | bytes 1540
  14.2 443.1 %reduce-scatter.2.cloned.1.call-start = ((), (), s32[]{:S(2)}) async-start(), calls=%async_computation.2 | async-start | bytes 9437184 | tf_op jit(solution)/shard_map/reduce_scatter | solution.py:374
  310.3 0.8 copy-start
Sparse Core Ops, SparseCore 0:
  14.4 127.6 all-gather.1
  310.5 146.8 reduce-scatter.1
